TPU v7x, 256 devices: a whole 4x4x8 slice. The times are simulated.
256 devices in a mesh: row: 4 (over x_lo, core), ang: 64 (over y, x_hi, z).
Axes of the slice: x: 4 (x_hi: 2, x_lo: 2; x = x_hi * 2 + x_lo), y: 4, z: 8, core: 2. Of those that a mesh axis runs over, the one named last changes fastest.
Arguments:
- linv_t: bfloat16 [2, 2048, 2048], P(None, 'ang', 'row'), may hold values from -1.5 to 1.5, as said below
- rhs_top: float32 [2, 2048, 32768], P(None, 'row', 'ang'), may hold values from -6 to 6
- factor_t: bfloat16 [2, 2048, 4096], P(None, 'ang', 'row'), may hold values from -0.125 to 0.125
- rhs_rest: float32 [2, 4096, 32768], P(None, 'row', 'ang'), may hold values from -6 to 6
Outputs:
- solved: float32 [2, 2048, 32768], P(None, 'row', 'ang')
- updated: float32 [2, 4096, 32768], P(None, 'row', 'ang')
Inputs may be any that keep to these rules, and one draw needn't show every extreme that they name: `linv_t`: lower triangular inverse: entry [c, j, i] is zero where j > i; the diagonal is real and between 0.5 and 1.5.
All inputs are finite; a program needn't handle non-finite values.
Results may differ from a plain program's by a relative error of at most 0.0026.
Values may be sent and summed in bfloat16 or wider, within the bound.
No kernel may reach another device: no remote copies, remote signals or barrier semaphores. Data moves between devices by JAX's collectives and lax.ppermute only.
A program may use at most 128 MiB of HBM per device.

v0:
```python
import jax
import jax.numpy as jnp
from jax import lax
from jax.sharding import Mesh
from jax.sharding import PartitionSpec as P

ANG = ("ang_0", "ang_1", "ang_2")


def laid_out(tiles, dim):
    dims = list(tiles.shape[1:])
    dims[dim] *= tiles.shape[0]
    return jnp.moveaxis(tiles, 0, dim).reshape(dims)


def gather_in_order(value, axes, sequence):
    tiles = value[None]
    for k in sequence:
        tiles = lax.all_gather(tiles, axes[k], axis=0, tiled=True)
    block = [lax.axis_size(axes[k]) for k in reversed(sequence)]
    tiles = tiles.reshape(*block, *value.shape)
    turned = sorted(range(len(sequence)), key=lambda place: sequence[len(sequence) - 1 - place])
    return tiles.transpose(*turned, *range(len(sequence), tiles.ndim)).reshape(-1, *value.shape)


def gather_axes(value, axes, sequence, dim):
    return laid_out(gather_in_order(value, axes, sequence), dim)


def complex_tdot(left, right, precision):
    dims = (((0,), (0,)), ((), ()))

    def single(first, second):
        return lax.dot_general(
            first, second, dims, precision=precision, preferred_element_type=jnp.float32
        )

    real_part = single(left[0], right[0]) - single(left[1], right[1])
    imag_part = single(left[0], right[1]) + single(left[1], right[0])
    return jnp.stack([real_part, imag_part])


def body(linv_t, rhs_top, factor_t, rhs_rest):
    top_all = lax.all_gather(rhs_top, "row", axis=1, tiled=True)
    solved = complex_tdot(
        gather_axes(linv_t, ANG, (1, 0, 2), 1).astype(jnp.float32), top_all, lax.Precision.HIGHEST
    )
    solved_half = solved.astype(jnp.bfloat16)
    solved_all = lax.all_gather(solved_half, "row", axis=1, tiled=True)
    update = complex_tdot(lax.all_gather(factor_t, ANG, axis=1, tiled=True), solved_all, None)
    return (solved, rhs_rest - update)


def solution(mesh):
    finer = Mesh(
        mesh.devices.reshape(mesh.shape["row"], 4, 2, 8), ("row", "ang_0", "ang_1", "ang_2")
    )
    placed = (P(None, ANG, "row"), P(None, "row", ANG), P(None, ANG, "row"), P(None, "row", ANG))
    return jax.shard_map(
        body,
        mesh=finer,
        in_specs=placed,
        out_specs=(P(None, "row", ANG), P(None, "row", ANG)),
        check_vma=False,
    )
```

profile of v0, /device:TPU:1, one launch (start us, length us, event | category | flops | bytes accessed | tf_op | source)
XLA Modules:
  0.0 401.9 jit_solution(10516816901624122911)
XLA Ops:
  7.2 0.0 all-gather.6.cloned.1.call-start
  7.2 6.2 %all-gather = bf16[4,32,512]{2,1,0:T(8,128)(2,1)S(1)} all-gather(bf16[2,32,512]{2,1,0:T(8,128)(2,1)} %param.4), channel_id=2, replica_groups=mesh['row'=4,'ang_0'=4,'ang_1'=2,'ang_2'=8] {'ang_1'}, dimensions={0}, use_global_device_ids=true | all-gather | bytes 196608 | tf_op jit(solution)/shard_map/all_gather | solution.py:19
  13.4 11.9 %all_gather.19 = bf16[8,2,32,512]{3,2,1,0:T(8,128)(2,1)} all-gather(bf16[2,2,32,512]{3,2,1,0:T(8,128)(2,1)S(1)} %bitcast.71), channel_id=1, replica_groups=mesh['row'=4,'ang_0'=4,'ang_1'=2,'ang_2'=8] {'ang_0'}, dimensions={0}, use_global_device_ids=true | all-gather | bytes 655360 | tf_op jit(solution)/shard_map/all_gather | solution.py:19
  25.3 0.0 all-gather.6.cloned.1.call-update
  25.3 0.0 all-gather.8.cloned.1.call-start
  25.4 0.7 all-gather.8.cloned.1.call-update
  26.1 0.0 all-gather.12.cloned.1.call-start
  26.1 0.7 all-gather.12.cloned.1.call-update
  26.8 0.0 all-gather.10.cloned.1.call-start
  26.9 59.5 %all-gather.6.cloned.1.call-done = bf16[64,2,32,512]{3,2,1,0:T(8,128)(2,1)} async-done(((bf16[8,2,32,512]{3,2,1,0:T(8,128)(2,1)}), bf16[64,2,32,512]{3,2,1,0:T(8,128)(2,1)}) %all-gather.6.cloned.1.call-update) | async-done | bytes 4194320 | tf_op jit(solution)/shard_map/all_gather | solution.py:19
  86.3 2.7 copy.13
  89.0 1.7 fusion.13
  90.7 80.4 %all-gather.8.cloned.1.call-done = f32[2,2048,512]{2,1,0:T(8,128)} async-done(((f32[2,512,512]{2,1,0:T(8,128)}), f32[2,2048,512]{2,1,0:T(8,128)}) %all-gather.8.cloned.1.call-update) | async-done | bytes 8388624 | tf_op jit(solution)/shard_map/all_gather | solution.py:44
  171.1 0.0 copy-start.1
  171.1 0.0 copy-start.3
  171.1 6.9 %fusion.1 = f32[512,512]{1,0:T(8,128)S(1)} fusion(bf16[2048,512]{1,0:T(8,128)(2,1)S(1)} %bitcast.67, f32[2,2048,512]{2,1,0:T(8,128)} %all-gather.8.cloned.1.call-done), kind=kOutput, calls=%fused_computation.6 | convolution fusion | flops 6442450944 | bytes 7340032 | tf_op jit(solution)/shard_map/dot_general | solution.py:34
  178.1 0.0 copy-done.1
  178.1 0.0 copy-done.3
  178.1 3.6 fusion
  181.7 3.6 fusion.9
  185.3 3.6 fusion.11
  188.9 2.1 fusion.12
  191.0 0.0 all-gather.10.cloned.1.call-update
  191.0 5.4 %copy.14 = f32[2,1024,512]{1,2,0:T(8,128)} copy(f32[2,1024,512]{2,1,0:T(8,128)} %param.7) | data formatting | bytes 8388608 | tf_op args[3]
  196.4 126.5 %all-gather.12.cloned.1.call-done = bf16[2,2048,1024]{2,1,0:T(8,128)(2,1)} async-done(((bf16[2,32,1024]{2,1,0:T(8,128)(2,1)}), bf16[2,2048,1024]{2,1,0:T(8,128)(2,1)}) %all-gather.12.cloned.1.call-update) | async-done | bytes 8388624 | tf_op jit(solution)/shard_map/all_gather | solution.py:50
  322.9 50.8 %all-gather.10.cloned.1.call-done = bf16[2,2048,512]{2,1,0:T(8,128)(2,1)} async-done(((bf16[2,512,512]{2,1,0:T(8,128)(2,1)}), bf16[2,2048,512]{2,1,0:T(8,128)(2,1)}) %all-gather.10.cloned.1.call-update) | async-done | bytes 4194320 | tf_op jit(solution)/shard_map/all_gather | solution.py:49
  373.7 0.0 copy-start.2
  373.7 0.0 copy-start.4
  373.7 5.3 %fusion.5 = f32[512,1024]{1,0:T(8,128)S(1)} fusion(bf16[2,2048,1024]{2,1,0:T(8,128)(2,1)} %all-gather.12.cloned.1.call-done, bf16[2,2048,512]{2,1,0:T(8,128)(2,1)} %all-gather.10.cloned.1.call-done), kind=kOutput, calls=%fused_computation.10 | convolution fusion | flops 2147483648 | bytes 8388608 | tf_op jit(solution)/shard_map/dot_general | solution.py:34
  379.0 0.0 copy-done.2
  379.0 1.1 copy-done.4
  380.1 2.3 fusion.4
  382.4 2.3 subtract_bitcast_fusion
  384.8 0.0 copy-start
  384.8 2.3 add_bitcast_fusion
  387.1 0.0 copy-done
  387.2 2.9 maximum_subtract_fusion
  390.0 5.4 %copy.15 = f32[2,1024,512]{2,1,0:T(8,128)} copy(f32[2,1024,512]{1,2,0:T(8,128)} %maximum_subtract_fusion) | data formatting | bytes 8388608
Async XLA Ops:
  7.2 79.2 %all-gather.6.cloned.1.call-start = ((), (), s32[]{:S(2)}) async-start(), calls=%async_computation | async-start | bytes 4718592 | tf_op jit(solution)/shard_map/all_gather | solution.py:19
  25.3 145.8 %all-gather.8.cloned.1.call-start = ((), (), s32[]{:S(2)}) async-start(), calls=%async_computation.1 | async-start | bytes 10485760 | tf_op jit(solution)/shard_map/all_gather | solution.py:44
  26.1 296.8 %all-gather.12.cloned.1.call-start = ((), (), s32[]{:S(2)}) async-start(), calls=%async_computation.3 | async-start | bytes 8519680 | tf_op jit(solution)/shard_map/all_gather | solution.py:50
  26.8 346.8 %all-gather.10.cloned.1.call-start = ((), (), s32[]{:S(2)}) async-start(), calls=%async_computation.2 | async-start | bytes 5242880 | tf_op jit(solution)/shard_map/all_gather | solution.py:49
  171.1 6.9 %copy-start.1 = (bf16[1,64,32,512]{3,2,0,1:T(8,128)(2,1)S(1)}, bf16[1,64,32,512]{3,2,0,1:T(8,128)(2,1)}, u32[]{:S(2)}) copy-start(bf16[1,64,32,512]{3,2,0,1:T(8,128)(2,1)} %get-tuple-element.13) | copy-start | bytes 6291460
  171.1 6.9 %copy-start.3 = (f32[2,2048,512]{2,1,0:T(8,128)S(1)}, f32[2,2048,512]{2,1,0:T(8,128)}, u32[]{:S(2)}) copy-start(f32[2,2048,512]{2,1,0:T(8,128)} %all-gather.8.cloned.1.call-done) | copy-start | bytes 25165828
  373.7 5.3 %copy-start.2 = (bf16[2,2048,1024]{2,1,0:T(8,128)(2,1)S(1)}, bf16[2,2048,1024]{2,1,0:T(8,128)(2,1)}, u32[]{:S(2)}) copy-start(bf16[2,2048,1024]{2,1,0:T(8,128)(2,1)} %all-gather.12.cloned.1.call-done) | copy-start | bytes 25165828
  373.7 6.4 %copy-start.4 = (bf16[2,2048,512]{2,1,0:T(8,128)(2,1)S(1)}, bf16[2,2048,512]{2,1,0:T(8,128)(2,1)}, u32[]{:S(2)}) copy-start(bf16[2,2048,512]{2,1,0:T(8,128)(2,1)} %all-gather.10.cloned.1.call-done) | copy-start | bytes 12582916
  384.8 2.4 copy-start
Sparse Core Ops, SparseCore 0:
  25.4 60.8 all-gather.5
  88.1 82.9 all-gather.7
  174.7 148.1 all-gather.11
  324.6 49.0 all-gather.9
where the time goes:
time: 402 us
  waiting for transfers between devices  319 us (79%)
  matrix products  30.1 us (7%)
  blocking collectives  18.1 us (5%)
  local copies, waits for them, and re-layouts  16.2 us (4%)
  between operations  13.9 us (3%)
  other arithmetic  4.99 us (1%)
    all_gather x1, waiting for transfers between devices, body(): lax.all_gather(factor_t, ANG, axis=1, tiled=True)  126 us
    all_gather x1, waiting for transfers between devices, body(): top_all = lax.all_gather(rhs_top, 'row', axis=1, tiled=True)  80.4 us
    all_gather x1, waiting for transfers between devices, gather_in_order(): tiles = lax.all_gather(tiles, axes[k], axis=0, tiled=True)  59.5 us
    all_gather x1, waiting for transfers between devices, body(): solved_all = lax.all_gather(solved_half, 'row', axis=1, tiled=True)  50.8 us
    dot_general x8, matrix products, single(): lax.dot_general(first, second, dims, precision=precision, preferred_eleme...  30.1 us
    all_gather x2, blocking collectives, gather_in_order(): tiles = lax.all_gather(tiles, axes[k], axis=0, tiled=True)  18.1 us
    unnamed x12, local copies, waits for them, and re-layouts  11.8 us
  transfers between devices with their start and end apart: 4, of which 4 were waited for; matrix products, arithmetic and copies ran while one was open for 7% of the time, Pallas kernels for 0%

commit v1 on v0

v1 whole, which is shorter than its diff:
```python
import math

import jax
import jax.numpy as jnp
from jax import lax
from jax.experimental import pallas as pl
from jax.experimental.pallas import tpu as pltpu
from jax.sharding import Mesh
from jax.sharding import PartitionSpec as P

L_A = 256
F_A = 512


def after(value, *earlier):
    return lax.optimization_barrier((value, *earlier))[0]


def shift(value, axis, step):
    n = lax.axis_size(axis)
    return lax.ppermute(value, axis, [(i, (i + step) % n) for i in range(n)])


def laid_out(pieces, dim, places):
    first = pieces[0]
    shape = (*first.shape[:dim], len(pieces), *first.shape[dim:])
    lead = (slice(None),) * dim

    def kernel(*refs):
        out = refs[len(pieces)]
        for i, at in enumerate(places()):
            out[(*lead, at)] = refs[i][...]

    size = 2 * math.prod(shape) * first.dtype.itemsize
    return pl.pallas_call(
        kernel,
        out_shape=jax.ShapeDtypeStruct(shape, first.dtype),
        in_specs=[pl.BlockSpec(memory_space=pltpu.VMEM)] * len(pieces),
        out_specs=pl.BlockSpec(memory_space=pltpu.VMEM),
        compiler_params=pltpu.CompilerParams(vmem_limit_bytes=16 << 20),
        cost_estimate=pl.CostEstimate(flops=0, bytes_accessed=size, transcendentals=0),
    )(*pieces)


def row_distance():
    r = 2 * lax.axis_index("xl") + lax.axis_index("core")
    y = lax.axis_index("y")
    return [r ^ lax.rem(y + o, 4) for o in range(4)]


def along_z():
    z = lax.axis_index("z")
    return [lax.rem(z + o, 8) for o in range(8)]


def ring(value, axis, far_up, holds=None):
    n = lax.axis_size(axis)
    held = {0: value}
    for k in range(1, n // 2 + 1):
        up, down = held[(n - k + 1) % n], held[k - 1]
        if k > 1:
            extra = () if holds is None else holds.get(k, ())
            up, down = lax.optimization_barrier((up, down, *extra))[:2]
        if k < n // 2 or far_up:
            held[n - k] = shift(up, axis, 1)
        if k < n // 2 or not far_up:
            held[k] = shift(down, axis, -1)
    return [held[k] for k in range(n)]


def beside(value, axis):
    return shift(value, axis, -1), shift(value, axis, 1)


def square(value, right, left, axis):
    far = jnp.stack([shift(left[0], axis, 1), shift(right[1], axis, -1)])
    return [value, right, far, left]


def over_row(value, hold=None):
    across = shift(value, "xl", 1)
    near = shift(value, "core", 1)
    if hold is not None:
        across = after(across, hold)
    return [value, near, across, shift(across, "core", 1)]


def tdot(left, right):
    return lax.dot_general(
        left, right, (((0,), (0,)), ((), ())), preferred_element_type=jnp.float32
    )


def pair_tdot(left, right):
    k, m = right.shape[0], left.shape[-1]
    return tdot(left[0].reshape(k, m), right), tdot(left[1].reshape(k, m), right)


def added(one, two):
    return one[0] + two[0], one[1] + two[1]


def combined(first, second):
    half = first.shape[1] // 2
    return first[:, :half] - second[:, half:], first[:, half:] + second[:, :half]


def body(linv_t, rhs_top, factor_t, rhs_rest):
    r = 2 * lax.axis_index("xl") + lax.axis_index("core")
    y, xh = lax.axis_index("y"), lax.axis_index("xh")
    wide = 2 * rhs_top.shape[2]
    scope = jax.named_scope

    def both_halves(own, other):
        low = jnp.where(xh == 0, own, other)
        return jnp.stack([low, jnp.where(xh == 0, other, own)], axis=1)

    def near_y(value):
        moved = [value, shift(value, "y", -1), shift(value, "y", 2), shift(value, "y", 1)]
        return laid_out(moved, 1, row_distance)

    with scope("panel_x"):
        own = jnp.concatenate([linv_t, factor_t], axis=2)
        both = both_halves(own, shift(own, "xh", 1))
    n_l = linv_t.shape[2]
    a_cols = jnp.concatenate([both[..., :L_A], both[..., n_l : n_l + F_A]], axis=3)
    b_cols = jnp.concatenate([both[..., L_A:n_l], both[..., n_l + F_A :]], axis=3)

    top = jnp.concatenate([rhs_top[0], rhs_top[1]], axis=1)
    top_high = lax.reduce_precision(top, 8, 7)
    top_low = (top - top_high).astype(jnp.bfloat16)
    with scope("top_row"):
        top_high = after(top_high.astype(jnp.bfloat16), both)

    with scope("b_z"):
        line = lax.all_gather(b_cols, "z", axis=2, tiled=True)
    with scope("a_y"):
        near = near_y(a_cols)
    own_l, own_f = line[..., : n_l - L_A], line[..., n_l - L_A :]
    with scope("inverse_b_y"):
        right_l, left_l = beside(own_l, "y")
    with scope("inverse_a_z"):
        holds = {3: (line,), 4: (right_l, left_l)}
        ring_l = ring(near[..., :L_A], "z", True, holds)
        a_l = laid_out(ring_l, 3, along_z)
    with scope("top_row"):
        tops = jnp.stack(over_row(top_high, ring_l[2]))
    with scope("inverse_b_y"):
        b_l = square(own_l, right_l, left_l, "y")
    with scope("factor_a_z"):
        a_f = lax.all_gather(after(near[..., L_A:], line), "z", axis=3, tiled=True)
    with scope("factor_b_y"):
        own_f = after(own_f, right_l, left_l)
        b_f = square(own_f, *beside(own_f, "y"), "y")

    place = [r ^ jnp.mod(y + o, 4) for o in range(4)]

    def times_a(whole, right):
        return pair_tdot(whole, right.reshape(-1, wide))

    def times_b(pieces, right):
        sums = None
        for o in (0, 1, 3, 2):
            mine = lax.dynamic_index_in_dim(right, place[o], 0, keepdims=False)
            term = pair_tdot(pieces[o], mine.reshape(-1, wide))
            sums = term if sums is None else added(sums, term)
        return sums

    def sent(parts, hold=None):
        half = jnp.concatenate([p.astype(jnp.bfloat16) for p in parts], axis=1)
        return jnp.stack(over_row(half, hold))

    with scope("solve_a"):
        own = pair_tdot(a_l[:, 0], top_low)
        solved_a = combined(*added(times_a(a_l, tops), own))
    with scope("solved_a_row"):
        half_a = sent(solved_a)
    with scope("solve_b"):
        own = lax.select_n(jnp.mod(r - y, 4), *b_l)
        own = pair_tdot(own, top_low)
        solved_b = combined(*added(times_b(b_l, tops), own))
    with scope("solved_b_row"):
        half_b = sent(solved_b, a_f)
    solved = jnp.stack([jnp.concatenate([solved_a[c], solved_b[c]], axis=0) for c in range(2)])
    halves = jnp.stack([half_a, half_b], axis=1)

    with scope("update_a"):
        update_a = combined(*times_a(a_f, halves))
    with scope("update_b"):
        update_b = combined(*times_b(b_f, halves))
    rest = [
        [rhs_rest[c, :F_A] - update_a[c], rhs_rest[c, F_A:] - update_b[c]] for c in range(2)
    ]
    return solved, jnp.stack([jnp.concatenate(part, axis=0) for part in rest])


def solution(mesh):
    axes = ("xl", "core", "y", "xh", "z")
    finer = Mesh(mesh.devices.reshape(2, 2, 4, 2, 8), axes)
    row, ang = axes[:2], axes[2:]
    placed = (P(None, ang, row), P(None, row, ang), P(None, ang, row), P(None, row, ang))
    return jax.shard_map(
        body,
        mesh=finer,
        in_specs=placed,
        out_specs=(P(None, row, ang), P(None, row, ang)),
        check_vma=False,
    )
```

time: 402 us -> 188 us (0.47)
  waiting for transfers between devices: 319 us -> 72.8 us
  starting transfers between devices: 0.16 us -> 43.5 us
  blocking collectives: 18.1 us -> 0 us
  other arithmetic: 4.99 us -> 17.4 us
  matrix products: 30.1 us -> 19.8 us
    all_gather x4 -> x2, waiting for transfers between devices: 317 us -> 0.01 us  [the longest x1 0.01 us: body(): line = lax.all_gather(b_cols, 'z', axis=2, tiled=True)]
    ppermute x0 -> x28, waiting for transfers between devices: none -> 72.8 us  [shift(): return lax.ppermute(value, axis, [(i, (i + step) % n) for i in range(n)])]
    ppermute x0 -> x28, starting transfers between devices: none -> 43.4 us  [shift(): return lax.ppermute(value, axis, [(i, (i + step) % n) for i in range(n)])]
    all_gather x2 -> x0, blocking collectives: 18.1 us -> none  [gather_in_order(): tiles = lax.all_gather(tiles, axes[k], axis=0, tiled=True)]
    another operation x0 -> x14, other arithmetic: none -> 12.1 us  [the longest x1 3.79 us: body(): tops = jnp.stack(over_row(top_high, ring_l[2]))]
    dot_general x8 -> x24, matrix products: 30.1 us -> 19.8 us  [tdot(): lax.dot_general(left, right, (((0,), (0,)), ((), ())), preferred_element_...]
    unnamed x12 -> x21, local copies, waits for them, and re-layouts: 11.8 us -> 5.28 us
    slice x1 -> x11, local copies, waits for them, and re-layouts: 1.73 us -> 7.63 us  [the longest x2 3.4 us: body(): own_l, own_f = (line[..., :n_l - L_A], line[..., n_l - L_A:])]
  transfers between devices with their start and end apart: 4 -> 30, of which waited for: 4 -> 13; matrix products, arithmetic and copies ran while one was open for 7% -> 17% of each run, Pallas kernels for 0% -> 0%
where the time goes in v1:
time: 188 us; the launch traced here: 185 us
  waiting for transfers between devices  72.8 us (39%)
  starting transfers between devices  43.5 us (23%)
  matrix products  19.8 us (11%)
  other arithmetic  17.4 us (9%)
  local copies, waits for them, and re-layouts  16.1 us (9%)
  between operations  14.7 us (8%)
    ppermute x28, waiting for transfers between devices, shift(): return lax.ppermute(value, axis, [(i, (i + step) % n) for i in range(n)])  72.8 us
    ppermute x28, starting transfers between devices, shift(): return lax.ppermute(value, axis, [(i, (i + step) % n) for i in range(n)])  43.4 us
    dot_general x24, matrix products, tdot(): lax.dot_general(left, right, (((0,), (0,)), ((), ())), preferred_element_...  19.8 us
    unnamed x21, local copies, waits for them, and re-layouts  5.28 us
    another operation x1, other arithmetic, body(): tops = jnp.stack(over_row(top_high, ring_l[2]))  3.79 us
  transfers between devices with their start and end apart: 30, of which 13 were waited for; matrix products, arithmetic and copies ran while one was open for 17% of the time, Pallas kernels for 0%

profile of v1, /device:TPU:1, one launch (start us, length us, event | category | flops | bytes accessed | tf_op | source)
XLA Modules:
  0.0 184.6 jit_solution(17015730043129177689)
XLA Ops:
  7.2 1.0 constant_dynamic-update-slice_fusion.1
  8.2 0.9 constant_dynamic-update-slice_fusion
  9.1 3.7 %collective-permute-start = (bf16[2,32,1536]{2,1,0:T(8,128)(2,1)S(1)}, bf16[2,32,1536]{2,1,0:T(8,128)(2,1)S(1)}, u32[]{:S(2)}, u32[]{:S(2)}) collective-permute-start(bf16[2,32,1536]{2,1,0:T(8,128)(2,1)S(1)} %constant_dynamic-update-slice_fusion), channel_id=1, source_target_pairs={{0,8},{8,0},{1,9},{9,1},{2,10},{10,2},{3,11},{11,3},{4,12},{12,4},... | collective-permute-start | bytes 589832 | tf_op jit(solution)/shard_map/panel_x/ppermute | solution.py:21
  12.8 3.6 %collective-permute-done = bf16[2,32,1536]{2,1,0:T(8,128)(2,1)S(1)} collective-permute-done((bf16[2,32,1536]{2,1,0:T(8,128)(2,1)S(1)}, bf16[2,32,1536]{2,1,0:T(8,128)(2,1)S(1)}, u32[]{:S(2)}, u32[]{:S(2)}) %collective-permute-start) | collective-permute-done | bytes 196640 | tf_op jit(solution)/shard_map/panel_x/ppermute | solution.py:21
  17.4 1.4 reduce-precision_convert_fusion
  18.8 2.2 %collective-permute-start.14 = (bf16[512,1024]{1,0:T(8,128)(2,1)}, bf16[512,1024]{1,0:T(8,128)(2,1)}, u32[]{:S(2)}, u32[]{:S(2)}) collective-permute-start(bf16[512,1024]{1,0:T(8,128)(2,1)} %get-tuple-element.17), channel_id=1, source_target_pairs={{0,128},{128,0},{1,129},{129,1},{2,130},{130,2},{3,131},{131,3},{4... | collective-permute-start | bytes 3145736 | tf_op jit(solution)/shard_map/top_row/ppermute | solution.py:21
  21.0 2.8 %collective-permute-start.1 = (bf16[2,2,32,768]{3,2,1,0:T(8,128)(2,1)S(1)}, bf16[2,2,32,768]{3,2,1,0:T(8,128)(2,1)S(1)}, u32[]{:S(2)}, u32[]{:S(2)}) collective-permute-start(bf16[2,2,32,768]{3,2,1,0:T(8,128)(2,1)S(1)} %pad_maximum_fusion.8.refs_0_), channel_id=1, source_target_pairs={{0,48},{16,0},{32,16},{48,32},{1,49},{17,1},{33,17},{49,33},{2,50}... | collective-permute-start | bytes 589832 | tf_op jit(solution)/shard_map/a_y/ppermute | solution.py:21
  24.8 3.5 %collective-permute-done.1.refs_1_ = bf16[2,2,32,768]{3,2,1,0:T(8,128)(2,1)S(1)} collective-permute-done((bf16[2,2,32,768]{3,2,1,0:T(8,128)(2,1)S(1)}, bf16[2,2,32,768]{3,2,1,0:T(8,128)(2,1)S(1)}, u32[]{:S(2)}, u32[]{:S(2)}) %collective-permute-start.1) | collective-permute-done | bytes 196640 | tf_op jit(solution)/shard_map/a_y/ppermute | solution.py:21
  28.3 1.6 collective-permute-done.2.refs_2_
  29.9 5.8 %collective-permute-done.3.refs_3_ = bf16[2,2,32,768]{3,2,1,0:T(8,128)(2,1)S(1)} collective-permute-done((bf16[2,2,32,768]{3,2,1,0:T(8,128)(2,1)S(1)}, bf16[2,2,32,768]{3,2,1,0:T(8,128)(2,1)S(1)}, u32[]{:S(2)}, u32[]{:S(2)}) %collective-permute-start.3) | collective-permute-done | bytes 196640 | tf_op jit(solution)/shard_map/a_y/ppermute | solution.py:21
  35.8 5.7 %collective-permute-start.4 = (bf16[2,4,2,32,256]{4,3,2,1,0:T(8,128)(2,1)S(1)}, bf16[2,4,2,32,256]{4,3,2,1,0:T(8,128)(2,1)S(1)}, u32[]{:S(2)}, u32[]{:S(2)}) collective-permute-start(bf16[2,4,2,32,256]{4,3,2,1,0:T(8,128)(2,1)S(1)} %slice.215.refs_0_), channel_id=1, source_target_pairs={{0,7},{1,0},{2,1},{3,2},{4,3},{5,4},{6,5},{7,6},{8,15},{9,8},{10,9... | collective-permute-start | bytes 786440 | tf_op jit(solution)/shard_map/inverse_a_z/ppermute | solution.py:21
  41.5 9.0 %collective-permute-done.4.refs_1_ = bf16[2,4,2,32,256]{4,3,2,1,0:T(8,128)(2,1)S(1)} collective-permute-done((bf16[2,4,2,32,256]{4,3,2,1,0:T(8,128)(2,1)S(1)}, bf16[2,4,2,32,256]{4,3,2,1,0:T(8,128)(2,1)S(1)}, u32[]{:S(2)}, u32[]{:S(2)}) %collective-permute-start.4) | collective-permute-done | bytes 262176 | tf_op jit(solution)/shard_map/inverse_a_z/ppermute | solution.py:21
  50.5 4.5 %collective-permute-done.5.refs_7_ = bf16[2,4,2,32,256]{4,3,2,1,0:T(8,128)(2,1)S(1)} collective-permute-done((bf16[2,4,2,32,256]{4,3,2,1,0:T(8,128)(2,1)S(1)}, bf16[2,4,2,32,256]{4,3,2,1,0:T(8,128)(2,1)S(1)}, u32[]{:S(2)}, u32[]{:S(2)}) %collective-permute-start.5) | collective-permute-done | bytes 262176 | tf_op jit(solution)/shard_map/inverse_a_z/ppermute | solution.py:21
  55.0 2.4 %collective-permute-start.13 = (bf16[512,1024]{1,0:T(8,128)(2,1)}, bf16[512,1024]{1,0:T(8,128)(2,1)}, u32[]{:S(2)}, u32[]{:S(2)}) collective-permute-start(bf16[512,1024]{1,0:T(8,128)(2,1)} %get-tuple-element.17), channel_id=1, source_target_pairs={{0,64},{64,0},{1,65},{65,1},{2,66},{66,2},{3,67},{67,3},{4,68},{68... | collective-permute-start | bytes 3145736 | tf_op jit(solution)/shard_map/top_row/ppermute | solution.py:21
  57.5 8.0 %collective-permute-done.6.refs_2_ = bf16[2,4,2,32,256]{4,3,2,1,0:T(8,128)(2,1)S(1)} collective-permute-done((bf16[2,4,2,32,256]{4,3,2,1,0:T(8,128)(2,1)S(1)}, bf16[2,4,2,32,256]{4,3,2,1,0:T(8,128)(2,1)S(1)}, u32[]{:S(2)}, u32[]{:S(2)}) %collective-permute-start.6) | collective-permute-done | bytes 262176 | tf_op jit(solution)/shard_map/inverse_a_z/ppermute | solution.py:21
  65.5 1.2 collective-permute-start.15
  67.5 2.0 %slice.220 = bf16[2,2,256,256]{3,2,1,0:T(8,128)(2,1)} slice(bf16[2,2,256,768]{3,2,1,0:T(8,128)(2,1)} %all-gather.3.cloned.1.call-done), slice={[0:2], [0:2], [0:256], [0:256]} | slice | bytes 1048576 | tf_op jit(solution)/shard_map/slice | solution.py:139
  69.5 1.5 collective-permute-start.11
  70.9 5.0 %collective-permute-done.7.refs_6_ = bf16[2,4,2,32,256]{4,3,2,1,0:T(8,128)(2,1)S(1)} collective-permute-done((bf16[2,4,2,32,256]{4,3,2,1,0:T(8,128)(2,1)S(1)}, bf16[2,4,2,32,256]{4,3,2,1,0:T(8,128)(2,1)S(1)}, u32[]{:S(2)}, u32[]{:S(2)}) %collective-permute-start.7) | collective-permute-done | bytes 262176 | tf_op jit(solution)/shard_map/inverse_a_z/ppermute | solution.py:21
  76.1 1.3 collective-permute-start.9
  77.4 3.8 %pad_maximum_fusion.1 = bf16[4,512,1024]{2,1,0:T(8,128)(2,1)} fusion(bf16[1,512,1024]{2,1,0:T(8,128)(2,1)} %bitcast.9, bf16[1,512,1024]{2,1,0:T(8,128)(2,1)} %bitcast.8, bf16[1,512,1024]{2,1,0:T(8,128)(2,1)} %bitcast.7, bf16[1,512,1024]{2,1,0:T(8,128)(2,1)} %bitcast.6), kind=kLoop, calls=%fused_computation.9 | loop fusion | flops 6291456 | bytes 8388608 | tf_op jit(solution)/shard_map/top_row/stack | solution.py:147
  81.2 1.4 slice.246
  82.7 1.6 fusion.88
  84.6 1.5 collective-permute-start.25
  86.5 1.1 fusion.89
  87.8 2.7 %collective-permute-start.17 = (bf16[2,256,256]{2,1,0:T(8,128)(2,1)S(1)}, bf16[2,256,256]{2,1,0:T(8,128)(2,1)S(1)}, u32[]{:S(2)}, u32[]{:S(2)}) collective-permute-start(bf16[2,256,256]{2,1,0:T(8,128)(2,1)S(1)} %get-tuple-element.60), channel_id=1, source_target_pairs={{0,48},{16,0},{32,16},{48,32},{1,49},{17,1},{33,17},{49,33},{2,50}... | collective-permute-start | bytes 786440 | tf_op jit(solution)/shard_map/inverse_b_y/ppermute | solution.py:21
  92.3 1.0 collective-permute-done.12.refs_4_
  94.6 1.3 convolution_add_fusion.3
  95.9 1.3 convolution_add_fusion.2
  97.4 1.0 fusion.74
  99.1 15.8 %collective-permute-done.16 = bf16[2,256,256]{2,1,0:T(8,128)(2,1)S(1)} collective-permute-done((bf16[2,256,256]{2,1,0:T(8,128)(2,1)S(1)}, bf16[2,256,256]{2,1,0:T(8,128)(2,1)S(1)}, u32[]{:S(2)}, u32[]{:S(2)}) %collective-permute-start.16) | collective-permute-done | bytes 262176 | tf_op jit(solution)/shard_map/inverse_b_y/ppermute | solution.py:21
  114.9 2.2 %collective-permute-start.18 = (bf16[256,1024]{1,0:T(8,128)(2,1)}, bf16[256,1024]{1,0:T(8,128)(2,1)}, u32[]{:S(2)}, u32[]{:S(2)}) collective-permute-start(bf16[256,1024]{1,0:T(8,128)(2,1)} %get-tuple-element.55), channel_id=1, source_target_pairs={{0,64},{64,0},{1,65},{65,1},{2,66},{66,2},{3,67},{67,3},{4,68},{68... | collective-permute-start | bytes 1572872 | tf_op jit(solution)/shard_map/solved_a_row/ppermute | solution.py:21
  117.1 1.2 fusion.48
  121.6 12.2 %collective-permute-start.22 = (bf16[256,1024]{1,0:T(8,128)(2,1)S(1)}, bf16[256,1024]{1,0:T(8,128)(2,1)S(1)}, u32[]{:S(2)}, u32[]{:S(2)}) collective-permute-start(bf16[256,1024]{1,0:T(8,128)(2,1)S(1)} %get-tuple-element.53), channel_id=1, source_target_pairs={{0,128},{128,0},{1,129},{129,1},{2,130},{130,2},{3,131},{131,3},{4... | collective-permute-start | bytes 1572872 | tf_op jit(solution)/shard_map/solved_b_row/ppermute | solution.py:21
  134.2 1.5 pad_maximum_fusion.4
  137.0 1.0 copy-done.1
  138.0 0.9 slice_bitcast_fusion.4
  138.8 7.5 %collective-permute-done.22 = bf16[256,1024]{1,0:T(8,128)(2,1)S(1)} collective-permute-done((bf16[256,1024]{1,0:T(8,128)(2,1)S(1)}, bf16[256,1024]{1,0:T(8,128)(2,1)S(1)}, u32[]{:S(2)}, u32[]{:S(2)}) %collective-permute-start.22) | collective-permute-done | bytes 524320 | tf_op jit(solution)/shard_map/solved_b_row/ppermute | solution.py:21
  146.3 0.9 collective-permute-start.23
  147.2 1.8 maximum_bitcast_fusion
  149.0 0.9 copy-done.7
  152.4 6.9 %collective-permute-done.27 = bf16[2,256,512]{2,1,0:T(8,128)(2,1)} collective-permute-done((bf16[2,256,512]{2,1,0:T(8,128)(2,1)}, bf16[2,256,512]{2,1,0:T(8,128)(2,1)}, u32[]{:S(2)}, u32[]{:S(2)}) %collective-permute-start.27) | collective-permute-done | bytes 524320 | tf_op jit(solution)/shard_map/factor_b_y/ppermute | solution.py:21
  159.3 1.8 fusion.99
  161.5 2.3 %fusion.96 = f32[512,1024]{1,0:T(8,128)S(1)} fusion(bf16[2048,512]{1,0:T(8,128)(2,1)S(1)} %bitcast.184, bf16[2048,1024]{1,0:T(8,128)(2,1)S(1)} %bitcast.181), kind=kOutput, calls=%fused_computation.145 | convolution fusion | flops 2147483648 | bytes 8388608 | tf_op jit(solution)/shard_map/update_a/dot_general | solution.py:89
  163.9 2.3 %fusion.97 = f32[512,1024]{1,0:T(8,128)S(1)} fusion(bf16[2048,512]{1,0:T(8,128)(2,1)S(1)} %bitcast.183, bf16[2048,1024]{1,0:T(8,128)(2,1)S(1)} %bitcast.182), kind=kOutput, calls=%fused_computation.146 | convolution fusion | flops 2147483648 | bytes 8388608 | tf_op jit(solution)/shard_map/update_a/dot_general | solution.py:89
  171.7 1.4 copy-done.8
  173.1 1.6 fusion.17
  175.1 2.5 %pad_maximum_fusion.2 = f32[2,1024,512]{2,1,0:T(8,128)} fusion(f32[1,1024,512]{2,1,0:T(8,128)S(1)} %get-tuple-element.73, f32[1,1024,512]{2,1,0:T(8,128)S(1)} %get-tuple-element.72), kind=kLoop, calls=%fused_computation.10 | loop fusion | flops 1048576 | bytes 8388608 | tf_op jit(solution)/shard_map/stack | solution.py:194
  (98 shorter events, 22.1 us)
Async XLA Ops:
  7.2 10.0 %copy-start.9 = (f32[2,512,512]{2,1,0:T(8,128)S(1)}, f32[2,512,512]{2,1,0:T(8,128)}, u32[]{:S(2)}) copy-start(f32[2,512,512]{2,1,0:T(8,128)} %param.5) | copy-start | bytes 6291460
  7.2 60.3 %all-gather.3.cloned.1.call-start = ((), (), s32[]{:S(2)}) async-start(), calls=%async_computation | async-start | bytes 1769472 | tf_op jit(solution)/shard_map/b_z/all_gather | solution.py:136
  9.1 7.2 %collective-permute-start = (bf16[2,32,1536]{2,1,0:T(8,128)(2,1)S(1)}, bf16[2,32,1536]{2,1,0:T(8,128)(2,1)S(1)}, u32[]{:S(2)}, u32[]{:S(2)}) collective-permute-start(bf16[2,32,1536]{2,1,0:T(8,128)(2,1)S(1)} %constant_dynamic-update-slice_fusion), channel_id=1, source_target_pairs={{0,8},{8,0},{1,9},{9,1},{2,10},{10,2},{3,11},{11,3},{4,12},{12,4},... | collective-permute-start | bytes 589832 | tf_op jit(solution)/shard_map/panel_x/ppermute | solution.py:21
  17.2 129.2 %all-gather.5.cloned.1.call-start = ((), (), s32[]{:S(2)}) async-start(), calls=%async_computation.1 | async-start | bytes 4718592 | tf_op jit(solution)/shard_map/factor_a_z/all_gather | solution.py:151
  18.8 46.7 %collective-permute-start.14 = (bf16[512,1024]{1,0:T(8,128)(2,1)}, bf16[512,1024]{1,0:T(8,128)(2,1)}, u32[]{:S(2)}, u32[]{:S(2)}) collective-permute-start(bf16[512,1024]{1,0:T(8,128)(2,1)} %get-tuple-element.17), channel_id=1, source_target_pairs={{0,128},{128,0},{1,129},{129,1},{2,130},{130,2},{3,131},{131,3},{4... | collective-permute-start | bytes 3145736 | tf_op jit(solution)/shard_map/top_row/ppermute | solution.py:21
  21.0 7.3 %collective-permute-start.1 = (bf16[2,2,32,768]{3,2,1,0:T(8,128)(2,1)S(1)}, bf16[2,2,32,768]{3,2,1,0:T(8,128)(2,1)S(1)}, u32[]{:S(2)}, u32[]{:S(2)}) collective-permute-start(bf16[2,2,32,768]{3,2,1,0:T(8,128)(2,1)S(1)} %pad_maximum_fusion.8.refs_0_), channel_id=1, source_target_pairs={{0,48},{16,0},{32,16},{48,32},{1,49},{17,1},{33,17},{49,33},{2,50}... | collective-permute-start | bytes 589832 | tf_op jit(solution)/shard_map/a_y/ppermute | solution.py:21
  23.8 6.1 %collective-permute-start.2 = (bf16[2,2,32,768]{3,2,1,0:T(8,128)(2,1)S(1)}, bf16[2,2,32,768]{3,2,1,0:T(8,128)(2,1)S(1)}, u32[]{:S(2)}, u32[]{:S(2)}) collective-permute-start(bf16[2,2,32,768]{3,2,1,0:T(8,128)(2,1)S(1)} %pad_maximum_fusion.8.refs_0_), channel_id=1, source_target_pairs={{0,32},{16,48},{32,0},{48,16},{1,33},{17,49},{33,1},{49,17},{2,34}... | collective-permute-start | bytes 589832 | tf_op jit(solution)/shard_map/a_y/ppermute | solution.py:21
  24.1 11.6 %collective-permute-start.3 = (bf16[2,2,32,768]{3,2,1,0:T(8,128)(2,1)S(1)}, bf16[2,2,32,768]{3,2,1,0:T(8,128)(2,1)S(1)}, u32[]{:S(2)}, u32[]{:S(2)}) collective-permute-start(bf16[2,2,32,768]{3,2,1,0:T(8,128)(2,1)S(1)} %pad_maximum_fusion.8.refs_0_), channel_id=1, source_target_pairs={{0,16},{16,32},{32,48},{48,0},{1,17},{17,33},{33,49},{49,1},{2,18}... | collective-permute-start | bytes 589832 | tf_op jit(solution)/shard_map/a_y/ppermute | solution.py:21
  35.8 14.7 %collective-permute-start.4 = (bf16[2,4,2,32,256]{4,3,2,1,0:T(8,128)(2,1)S(1)}, bf16[2,4,2,32,256]{4,3,2,1,0:T(8,128)(2,1)S(1)}, u32[]{:S(2)}, u32[]{:S(2)}) collective-permute-start(bf16[2,4,2,32,256]{4,3,2,1,0:T(8,128)(2,1)S(1)} %slice.215.refs_0_), channel_id=1, source_target_pairs={{0,7},{1,0},{2,1},{3,2},{4,3},{5,4},{6,5},{7,6},{8,15},{9,8},{10,9... | collective-permute-start | bytes 786440 | tf_op jit(solution)/shard_map/inverse_a_z/ppermute | solution.py:21
  41.5 13.6 %collective-permute-start.5 = (bf16[2,4,2,32,256]{4,3,2,1,0:T(8,128)(2,1)S(1)}, bf16[2,4,2,32,256]{4,3,2,1,0:T(8,128)(2,1)S(1)}, u32[]{:S(2)}, u32[]{:S(2)}) collective-permute-start(bf16[2,4,2,32,256]{4,3,2,1,0:T(8,128)(2,1)S(1)} %slice.215.refs_0_), channel_id=1, source_target_pairs={{0,1},{1,2},{2,3},{3,4},{4,5},{5,6},{6,7},{7,0},{8,9},{9,10},{10,1... | collective-permute-start | bytes 786440 | tf_op jit(solution)/shard_map/inverse_a_z/ppermute | solution.py:21
  55.0 10.4 %collective-permute-start.6 = (bf16[2,4,2,32,256]{4,3,2,1,0:T(8,128)(2,1)S(1)}, bf16[2,4,2,32,256]{4,3,2,1,0:T(8,128)(2,1)S(1)}, u32[]{:S(2)}, u32[]{:S(2)}) collective-permute-start(bf16[2,4,2,32,256]{4,3,2,1,0:T(8,128)(2,1)S(1)} %collective-permute-done.4.refs_1_), channel_id=1, source_target_pairs={{0,7},{1,0},{2,1},{3,2},{4,3},{5,4},{6,5},{7,6},{8,15},{9,8},{10,9... | collective-permute-start | bytes 786440 | tf_op jit(solution)/shard_map/inverse_a_z/ppermute | solution.py:21
  55.0 21.0 %collective-permute-start.13 = (bf16[512,1024]{1,0:T(8,128)(2,1)}, bf16[512,1024]{1,0:T(8,128)(2,1)}, u32[]{:S(2)}, u32[]{:S(2)}) collective-permute-start(bf16[512,1024]{1,0:T(8,128)(2,1)} %get-tuple-element.17), channel_id=1, source_target_pairs={{0,64},{64,0},{1,65},{65,1},{2,66},{66,2},{3,67},{67,3},{4,68},{68... | collective-permute-start | bytes 3145736 | tf_op jit(solution)/shard_map/top_row/ppermute | solution.py:21
  65.5 11.9 %collective-permute-start.15 = (bf16[512,1024]{1,0:T(8,128)(2,1)}, bf16[512,1024]{1,0:T(8,128)(2,1)}, u32[]{:S(2)}, u32[]{:S(2)}) collective-permute-start(bf16[512,1024]{1,0:T(8,128)(2,1)} %collective-permute-done.14), channel_id=1, source_target_pairs={{0,64},{64,0},{1,65},{65,1},{2,66},{66,2},{3,67},{67,3},{4,68},{68... | collective-permute-start | bytes 3145736 | tf_op jit(solution)/shard_map/top_row/ppermute | solution.py:21
  66.7 9.3 %collective-permute-start.7 = (bf16[2,4,2,32,256]{4,3,2,1,0:T(8,128)(2,1)S(1)}, bf16[2,4,2,32,256]{4,3,2,1,0:T(8,128)(2,1)S(1)}, u32[]{:S(2)}, u32[]{:S(2)}) collective-permute-start(bf16[2,4,2,32,256]{4,3,2,1,0:T(8,128)(2,1)S(1)} %collective-permute-done.5.refs_7_), channel_id=1, source_target_pairs={{0,1},{1,2},{2,3},{3,4},{4,5},{5,6},{6,7},{7,0},{8,9},{9,10},{10,1... | collective-permute-start | bytes 786440 | tf_op jit(solution)/shard_map/inverse_a_z/ppermute | solution.py:21
  69.5 14.8 %collective-permute-start.10 = (bf16[2,2,256,256]{3,2,1,0:T(8,128)(2,1)}, bf16[2,2,256,256]{3,2,1,0:T(8,128)(2,1)S(1)}, u32[]{:S(2)}, u32[]{:S(2)}) collective-permute-start(bf16[2,2,256,256]{3,2,1,0:T(8,128)(2,1)} %slice.220), channel_id=1, source_target_pairs={{0,48},{16,0},{32,16},{48,32},{1,49},{17,1},{33,17},{49,33},{2,50}... | collective-permute-start | bytes 1572872 | tf_op jit(solution)/shard_map/inverse_b_y/ppermute | solution.py:21
  69.5 14.8 %collective-permute-start.11 = (bf16[2,2,256,256]{3,2,1,0:T(8,128)(2,1)}, bf16[2,2,256,256]{3,2,1,0:T(8,128)(2,1)}, u32[]{:S(2)}, u32[]{:S(2)}) collective-permute-start(bf16[2,2,256,256]{3,2,1,0:T(8,128)(2,1)} %slice.220), channel_id=1, source_target_pairs={{0,16},{16,32},{32,48},{48,0},{1,17},{17,33},{33,49},{49,1},{2,18}... | collective-permute-start | bytes 1572872 | tf_op jit(solution)/shard_map/inverse_b_y/ppermute | solution.py:21
  75.9 10.1 %collective-permute-start.8 = (bf16[2,4,2,32,256]{4,3,2,1,0:T(8,128)(2,1)S(1)}, bf16[2,4,2,32,256]{4,3,2,1,0:T(8,128)(2,1)S(1)}, u32[]{:S(2)}, u32[]{:S(2)}) collective-permute-start(bf16[2,4,2,32,256]{4,3,2,1,0:T(8,128)(2,1)S(1)} %collective-permute-done.6.refs_2_), channel_id=1, source_target_pairs={{0,7},{1,0},{2,1},{3,2},{4,3},{5,4},{6,5},{7,6},{8,15},{9,8},{10,9... | collective-permute-start | bytes 786440 | tf_op jit(solution)/shard_map/inverse_a_z/ppermute | solution.py:21
  76.1 10.0 %collective-permute-start.9 = (bf16[2,4,2,32,256]{4,3,2,1,0:T(8,128)(2,1)S(1)}, bf16[2,4,2,32,256]{4,3,2,1,0:T(8,128)(2,1)S(1)}, u32[]{:S(2)}, u32[]{:S(2)}) collective-permute-start(bf16[2,4,2,32,256]{4,3,2,1,0:T(8,128)(2,1)S(1)} %collective-permute-done.7.refs_6_), channel_id=1, source_target_pairs={{0,1},{1,2},{2,3},{3,4},{4,5},{5,6},{6,7},{7,0},{8,9},{9,10},{10,1... | collective-permute-start | bytes 786440 | tf_op jit(solution)/shard_map/inverse_a_z/ppermute | solution.py:21
  81.2 9.2 %copy-start = (bf16[4,512,1024]{2,1,0:T(8,128)(2,1)S(1)}, bf16[4,512,1024]{2,1,0:T(8,128)(2,1)}, u32[]{:S(2)}) copy-start(bf16[4,512,1024]{2,1,0:T(8,128)(2,1)} %pad_maximum_fusion.1) | copy-start | bytes 12582916
  82.7 8.2 %copy-start.5 = (bf16[2,2,256,512]{3,2,1,0:T(8,128)(2,1)}, bf16[2,2,256,512]{3,2,1,0:T(8,128)(2,1)S(1)}, u32[]{:S(2)}) copy-start(bf16[2,2,256,512]{3,2,1,0:T(8,128)(2,1)S(1)} %slice.246) | copy-start | bytes 3145732
  84.2 52.7 %collective-permute-start.24 = (bf16[2,2,256,512]{3,2,1,0:T(8,128)(2,1)S(1)}, bf16[2,2,256,512]{3,2,1,0:T(8,128)(2,1)S(1)}, u32[]{:S(2)}, u32[]{:S(2)}) collective-permute-start(bf16[2,2,256,512]{3,2,1,0:T(8,128)(2,1)S(1)} %slice.246), channel_id=1, source_target_pairs={{0,48},{16,0},{32,16},{48,32},{1,49},{17,1},{33,17},{49,33},{2,50}... | collective-permute-start | bytes 3145736 | tf_op jit(solution)/shard_map/factor_b_y/ppermute | solution.py:21
  84.6 51.1 %collective-permute-start.25 = (bf16[2,2,256,512]{3,2,1,0:T(8,128)(2,1)S(1)}, bf16[2,2,256,512]{3,2,1,0:T(8,128)(2,1)S(1)}, u32[]{:S(2)}, u32[]{:S(2)}) collective-permute-start(bf16[2,2,256,512]{3,2,1,0:T(8,128)(2,1)S(1)} %slice.246), channel_id=1, source_target_pairs={{0,16},{16,32},{32,48},{48,0},{1,17},{17,33},{33,49},{49,1},{2,18}... | collective-permute-start | bytes 3145736 | tf_op jit(solution)/shard_map/factor_b_y/ppermute | solution.py:21
  86.1 7.2 %collective-permute-start.12 = (bf16[2,4,2,32,256]{4,3,2,1,0:T(8,128)(2,1)S(1)}, bf16[2,4,2,32,256]{4,3,2,1,0:T(8,128)(2,1)S(1)}, u32[]{:S(2)}, u32[]{:S(2)}) collective-permute-start(bf16[2,4,2,32,256]{4,3,2,1,0:T(8,128)(2,1)S(1)} %collective-permute-done.9.refs_5_), channel_id=1, source_target_pairs={{0,1},{1,2},{2,3},{3,4},{4,5},{5,6},{6,7},{7,0},{8,9},{9,10},{10,1... | collective-permute-start | bytes 786440 | tf_op jit(solution)/shard_map/inverse_a_z/ppermute | solution.py:21
  87.5 27.3 %collective-permute-start.16 = (bf16[2,256,256]{2,1,0:T(8,128)(2,1)S(1)}, bf16[2,256,256]{2,1,0:T(8,128)(2,1)S(1)}, u32[]{:S(2)}, u32[]{:S(2)}) collective-permute-start(bf16[2,256,256]{2,1,0:T(8,128)(2,1)S(1)} %get-tuple-element.57), channel_id=1, source_target_pairs={{0,16},{16,32},{32,48},{48,0},{1,17},{17,33},{33,49},{49,1},{2,18}... | collective-permute-start | bytes 786440 | tf_op jit(solution)/shard_map/inverse_b_y/ppermute | solution.py:21
  87.8 29.3 %collective-permute-start.17 = (bf16[2,256,256]{2,1,0:T(8,128)(2,1)S(1)}, bf16[2,256,256]{2,1,0:T(8,128)(2,1)S(1)}, u32[]{:S(2)}, u32[]{:S(2)}) collective-permute-start(bf16[2,256,256]{2,1,0:T(8,128)(2,1)S(1)} %get-tuple-element.60), channel_id=1, source_target_pairs={{0,48},{16,0},{32,16},{48,32},{1,49},{17,1},{33,17},{49,33},{2,50}... | collective-permute-start | bytes 786440 | tf_op jit(solution)/shard_map/inverse_b_y/ppermute | solution.py:21
  98.5 35.6 %collective-permute-start.19 = (bf16[256,1024]{1,0:T(8,128)(2,1)}, bf16[256,1024]{1,0:T(8,128)(2,1)}, u32[]{:S(2)}, u32[]{:S(2)}) collective-permute-start(bf16[256,1024]{1,0:T(8,128)(2,1)} %get-tuple-element.55), channel_id=1, source_target_pairs={{0,128},{128,0},{1,129},{129,1},{2,130},{130,2},{3,131},{131,3},{4... | collective-permute-start | bytes 1572872 | tf_op jit(solution)/shard_map/solved_a_row/ppermute | solution.py:21
  114.9 31.4 %collective-permute-start.18 = (bf16[256,1024]{1,0:T(8,128)(2,1)}, bf16[256,1024]{1,0:T(8,128)(2,1)}, u32[]{:S(2)}, u32[]{:S(2)}) collective-permute-start(bf16[256,1024]{1,0:T(8,128)(2,1)} %get-tuple-element.55), channel_id=1, source_target_pairs={{0,64},{64,0},{1,65},{65,1},{2,66},{66,2},{3,67},{67,3},{4,68},{68... | collective-permute-start | bytes 1572872 | tf_op jit(solution)/shard_map/solved_a_row/ppermute | solution.py:21
  121.6 24.7 %collective-permute-start.22 = (bf16[256,1024]{1,0:T(8,128)(2,1)S(1)}, bf16[256,1024]{1,0:T(8,128)(2,1)S(1)}, u32[]{:S(2)}, u32[]{:S(2)}) collective-permute-start(bf16[256,1024]{1,0:T(8,128)(2,1)S(1)} %get-tuple-element.53), channel_id=1, source_target_pairs={{0,128},{128,0},{1,129},{129,1},{2,130},{130,2},{3,131},{131,3},{4... | collective-permute-start | bytes 1572872 | tf_op jit(solution)/shard_map/solved_b_row/ppermute | solution.py:21
  134.0 13.2 %collective-permute-start.20 = (bf16[256,1024]{1,0:T(8,128)(2,1)}, bf16[256,1024]{1,0:T(8,128)(2,1)}, u32[]{:S(2)}, u32[]{:S(2)}) collective-permute-start(bf16[256,1024]{1,0:T(8,128)(2,1)} %collective-permute-done.19), channel_id=1, source_target_pairs={{0,64},{64,0},{1,65},{65,1},{2,66},{66,2},{3,67},{67,3},{4,68},{68... | collective-permute-start | bytes 1572872 | tf_op jit(solution)/shard_map/solved_a_row/ppermute | solution.py:21
  135.7 3.1 %copy-start.3 = (bf16[2,2,256,512]{3,2,1,0:T(8,128)(2,1)}, bf16[2,2,256,512]{3,2,1,0:T(8,128)(2,1)S(1)}, u32[]{:S(2)}) copy-start(bf16[2,2,256,512]{3,2,1,0:T(8,128)(2,1)S(1)} %collective-permute-done.25) | copy-start | bytes 3145732
  135.7 14.5 %collective-permute-start.21 = (bf16[256,1024]{1,0:T(8,128)(2,1)S(1)}, bf16[256,1024]{1,0:T(8,128)(2,1)S(1)}, u32[]{:S(2)}, u32[]{:S(2)}) collective-permute-start(bf16[256,1024]{1,0:T(8,128)(2,1)S(1)} %get-tuple-element.53), channel_id=1, source_target_pairs={{0,64},{64,0},{1,65},{65,1},{2,66},{66,2},{3,67},{67,3},{4,68},{68... | collective-permute-start | bytes 1572872 | tf_op jit(solution)/shard_map/solved_b_row/ppermute | solution.py:21
  137.0 1.0 copy-start.1
  137.0 14.7 %collective-permute-start.26 = (bf16[2,256,512]{2,1,0:T(8,128)(2,1)}, bf16[2,256,512]{2,1,0:T(8,128)(2,1)S(1)}, u32[]{:S(2)}, u32[]{:S(2)}) collective-permute-start(bf16[2,256,512]{2,1,0:T(8,128)(2,1)} %slice_bitcast_fusion.5), channel_id=1, source_target_pairs={{0,16},{16,32},{32,48},{48,0},{1,17},{17,33},{33,49},{49,1},{2,18}... | collective-permute-start | bytes 1572872 | tf_op jit(solution)/shard_map/factor_b_y/ppermute | solution.py:21
  146.3 13.0 %collective-permute-start.27 = (bf16[2,256,512]{2,1,0:T(8,128)(2,1)}, bf16[2,256,512]{2,1,0:T(8,128)(2,1)}, u32[]{:S(2)}, u32[]{:S(2)}) collective-permute-start(bf16[2,256,512]{2,1,0:T(8,128)(2,1)} %slice_bitcast_fusion.4), channel_id=1, source_target_pairs={{0,48},{16,0},{32,16},{48,32},{1,49},{17,1},{33,17},{49,33},{2,50}... | collective-permute-start | bytes 1572872 | tf_op jit(solution)/shard_map/factor_b_y/ppermute | solution.py:21
  146.3 3.9 %collective-permute-start.23 = (bf16[256,1024]{1,0:T(8,128)(2,1)S(1)}, bf16[256,1024]{1,0:T(8,128)(2,1)S(1)}, u32[]{:S(2)}, u32[]{:S(2)}) collective-permute-start(bf16[256,1024]{1,0:T(8,128)(2,1)S(1)} %collective-permute-done.22), channel_id=1, source_target_pairs={{0,64},{64,0},{1,65},{65,1},{2,66},{66,2},{3,67},{67,3},{4,68},{68... | collective-permute-start | bytes 1572872 | tf_op jit(solution)/shard_map/solved_b_row/ppermute | solution.py:21
  147.2 2.7 %copy-start.7 = (bf16[2,4,2,256,512]{4,3,2,1,0:T(8,128)(2,1)S(1)}, bf16[2,4,2,256,512]{4,3,2,1,0:T(8,128)(2,1)}, u32[]{:S(2)}) copy-start(bf16[2,4,2,256,512]{4,3,2,1,0:T(8,128)(2,1)} %all-gather.5.cloned.1.call-done) | copy-start | bytes 12582916
  163.9 2.4 %copy-start.2 = (bf16[2,2,256,512]{3,2,1,0:T(8,128)(2,1)S(1)}, bf16[2,2,256,512]{3,2,1,0:T(8,128)(2,1)}, u32[]{:S(2)}) copy-start(bf16[2,2,256,512]{3,2,1,0:T(8,128)(2,1)} %copy-done.1) | copy-start | bytes 3145732
  166.2 1.2 copy-start.4
  167.5 1.2 copy-start.6
  170.9 2.2 %copy-start.8 = (f32[2,1024,512]{2,1,0:T(8,128)S(1)}, f32[2,1024,512]{2,1,0:T(8,128)}, u32[]{:S(2)}) copy-start(f32[2,1024,512]{2,1,0:T(8,128)} %param.7) | copy-start | bytes 12582916
Sparse Core Ops, SparseCore 0:
  17.3 44.7 all-gather.2
  81.3 54.1 all-gather.4

commit v2 on v1

--- a/solution.py
+++ b/solution.py
@@ -10,6 +10,23 @@
 
 L_A = 256
 F_A = 512
+
+
+def gated(values, *earlier):
+    n = len(values)
+
+    def kernel(*refs):
+        pass
+
+    anywhere = pl.BlockSpec(memory_space=pl.ANY)
+    return pl.pallas_call(
+        kernel,
+        out_shape=[jax.ShapeDtypeStruct(v.shape, v.dtype) for v in values],
+        in_specs=[anywhere] * (n + len(earlier)),
+        out_specs=[anywhere] * n,
+        input_output_aliases={i: i for i in range(n)},
+        cost_estimate=pl.CostEstimate(flops=0, bytes_accessed=0, transcendentals=0),
+    )(*values, *earlier)
 
 
 def after(value, *earlier):
@@ -73,7 +90,7 @@
 
 
 def square(value, right, left, axis):
-    far = jnp.stack([shift(left[0], axis, 1), shift(right[1], axis, -1)])
+    far = shift(left[0], axis, 1), shift(right[1], axis, -1)
     return [value, right, far, left]
 
 
@@ -92,7 +109,7 @@
 
 
 def pair_tdot(left, right):
-    k, m = right.shape[0], left.shape[-1]
+    k, m = right.shape[0], left[0].shape[-1]
     return tdot(left[0].reshape(k, m), right), tdot(left[1].reshape(k, m), right)
 
 
@@ -158,11 +175,15 @@
     def times_a(whole, right):
         return pair_tdot(whole, right.reshape(-1, wide))
 
-    def times_b(pieces, right):
+    def times_b(pieces, right, *earlier):
         sums = None
         for o in (0, 1, 3, 2):
             mine = lax.dynamic_index_in_dim(right, place[o], 0, keepdims=False)
-            term = pair_tdot(pieces[o], mine.reshape(-1, wide))
+            piece = pieces[o]
+            if o == 2 and earlier:
+                corners = [v[:8, :128] for v in (*sums, *earlier)]
+                piece = tuple(gated(piece, *corners))
+            term = pair_tdot(piece, mine.reshape(-1, wide))
             sums = term if sums is None else added(sums, term)
         return sums
 
@@ -176,7 +197,9 @@
     with scope("solved_a_row"):
         half_a = sent(solved_a)
     with scope("solve_b"):
-        own = lax.select_n(jnp.mod(r - y, 4), *b_l)
+        own = tuple(
+            lax.select_n(jnp.mod(r - y, 4), *[piece[c] for piece in b_l]) for c in range(2)
+        )
         own = pair_tdot(own, top_low)
         solved_b = combined(*added(times_b(b_l, tops), own))
     with scope("solved_b_row"):
@@ -185,9 +208,10 @@
     halves = jnp.stack([half_a, half_b], axis=1)
 
     with scope("update_a"):
-        update_a = combined(*times_a(a_f, halves))
+        sums_a = times_a(a_f, halves)
+        update_a = combined(*sums_a)
     with scope("update_b"):
-        update_b = combined(*times_b(b_f, halves))
+        update_b = combined(*times_b(b_f, halves, *sums_a))
     rest = [
         [rhs_rest[c, :F_A] - update_a[c], rhs_rest[c, F_A:] - update_b[c]] for c in range(2)
     ]

time: 188 us -> 188 us (level)
  waiting for transfers between devices: 72.8 us -> 50.3 us
  starting transfers between devices: 43.5 us -> 61.1 us
  local copies, waits for them, and re-layouts: 16.1 us -> 18.9 us
  matrix products: 19.8 us -> 21.8 us
    ppermute x28, waiting for transfers between devices: 72.8 us -> 50.2 us  [shift(): return lax.ppermute(value, axis, [(i, (i + step) % n) for i in range(n)])]
    ppermute x28, starting transfers between devices: 43.4 us -> 61 us  [shift(): return lax.ppermute(value, axis, [(i, (i + step) % n) for i in range(n)])]
    slice x0 -> x5, local copies, waits for them, and re-layouts: none -> 2.85 us  [the longest x4 2.49 us: times_b(): corners = [v[:8, :128] for v in (*sums, *earlier)]]
    dot_general x24, matrix products: 19.8 us -> 21.8 us  [tdot(): lax.dot_general(left, right, (((0,), (0,)), ((), ())), preferred_element_...]
    unnamed x21 -> x31, local copies, waits for them, and re-layouts: 5.28 us -> 6.04 us
  transfers between devices with their start and end apart: 30 -> 30, of which waited for: 13 -> 11; matrix products, arithmetic and copies ran while one was open for 17% -> 22% of each run, Pallas kernels for 0% -> 0%
where the time goes in v2:
time: 188 us; the launch traced here: 184 us
  starting transfers between devices  61.1 us (32%)
  waiting for transfers between devices  50.3 us (27%)
  matrix products  21.8 us (12%)
  local copies, waits for them, and re-layouts  18.9 us (10%)
  other arithmetic  17.3 us (9%)
  between operations  14.7 us (8%)
    ppermute x28, starting transfers between devices, shift(): return lax.ppermute(value, axis, [(i, (i + step) % n) for i in range(n)])  61 us
    ppermute x28, waiting for transfers between devices, shift(): return lax.ppermute(value, axis, [(i, (i + step) % n) for i in range(n)])  50.2 us
    dot_general x24, matrix products, tdot(): lax.dot_general(left, right, (((0,), (0,)), ((), ())), preferred_element_...  21.8 us
    unnamed x31, local copies, waits for them, and re-layouts  6.04 us
    another operation x1, other arithmetic, body(): tops = jnp.stack(over_row(top_high, ring_l[2]))  3.79 us
  transfers between devices with their start and end apart: 30, of which 11 were waited for; matrix products, arithmetic and copies ran while one was open for 22% of the time, Pallas kernels for 0%

profile of v2, /device:TPU:1, one launch (start us, length us, event | category | flops | bytes accessed | tf_op | source)
XLA Modules:
  0.0 184.4 jit_solution(14569037339506755356)
XLA Ops:
  7.2 1.0 constant_dynamic-update-slice_fusion.1
  9.1 3.7 %collective-permute-start = (bf16[2,32,1536]{2,1,0:T(8,128)(2,1)S(1)}, bf16[2,32,1536]{2,1,0:T(8,128)(2,1)S(1)}, u32[]{:S(2)}, u32[]{:S(2)}) collective-permute-start(bf16[2,32,1536]{2,1,0:T(8,128)(2,1)S(1)} %constant_dynamic-update-slice_fusion), channel_id=1, source_target_pairs={{0,8},{8,0},{1,9},{9,1},{2,10},{10,2},{3,11},{11,3},{4,12},{12,4},... | collective-permute-start | bytes 589832 | tf_op jit(solution)/shard_map/panel_x/ppermute | solution.py:38
  12.8 3.6 %collective-permute-done = bf16[2,32,1536]{2,1,0:T(8,128)(2,1)S(1)} collective-permute-done((bf16[2,32,1536]{2,1,0:T(8,128)(2,1)S(1)}, bf16[2,32,1536]{2,1,0:T(8,128)(2,1)S(1)}, u32[]{:S(2)}, u32[]{:S(2)}) %collective-permute-start) | collective-permute-done | bytes 196640 | tf_op jit(solution)/shard_map/panel_x/ppermute | solution.py:38
  17.4 1.4 reduce-precision_convert_fusion
  18.8 2.2 %collective-permute-start.14 = (bf16[512,1024]{1,0:T(8,128)(2,1)}, bf16[512,1024]{1,0:T(8,128)(2,1)}, u32[]{:S(2)}, u32[]{:S(2)}) collective-permute-start(bf16[512,1024]{1,0:T(8,128)(2,1)} %get-tuple-element.19), channel_id=1, source_target_pairs={{0,128},{128,0},{1,129},{129,1},{2,130},{130,2},{3,131},{131,3},{4... | collective-permute-start | bytes 3145736 | tf_op jit(solution)/shard_map/top_row/ppermute | solution.py:38
  21.0 2.8 %collective-permute-start.1 = (bf16[2,2,32,768]{3,2,1,0:T(8,128)(2,1)S(1)}, bf16[2,2,32,768]{3,2,1,0:T(8,128)(2,1)S(1)}, u32[]{:S(2)}, u32[]{:S(2)}) collective-permute-start(bf16[2,2,32,768]{3,2,1,0:T(8,128)(2,1)S(1)} %pad_maximum_fusion.8.refs_0_), channel_id=1, source_target_pairs={{0,48},{16,0},{32,16},{48,32},{1,49},{17,1},{33,17},{49,33},{2,50}... | collective-permute-start | bytes 589832 | tf_op jit(solution)/shard_map/a_y/ppermute | solution.py:38
  24.8 3.5 %collective-permute-done.1.refs_1_ = bf16[2,2,32,768]{3,2,1,0:T(8,128)(2,1)S(1)} collective-permute-done((bf16[2,2,32,768]{3,2,1,0:T(8,128)(2,1)S(1)}, bf16[2,2,32,768]{3,2,1,0:T(8,128)(2,1)S(1)}, u32[]{:S(2)}, u32[]{:S(2)}) %collective-permute-start.1) | collective-permute-done | bytes 196640 | tf_op jit(solution)/shard_map/a_y/ppermute | solution.py:38
  28.3 1.6 collective-permute-done.2.refs_2_
  29.9 5.8 %collective-permute-done.3.refs_3_ = bf16[2,2,32,768]{3,2,1,0:T(8,128)(2,1)S(1)} collective-permute-done((bf16[2,2,32,768]{3,2,1,0:T(8,128)(2,1)S(1)}, bf16[2,2,32,768]{3,2,1,0:T(8,128)(2,1)S(1)}, u32[]{:S(2)}, u32[]{:S(2)}) %collective-permute-start.3) | collective-permute-done | bytes 196640 | tf_op jit(solution)/shard_map/a_y/ppermute | solution.py:38
  35.8 1.7 collective-permute-start.5
  37.5 4.0 %collective-permute-start.4 = (bf16[2,4,2,32,256]{4,3,2,1,0:T(8,128)(2,1)S(1)}, bf16[2,4,2,32,256]{4,3,2,1,0:T(8,128)(2,1)S(1)}, u32[]{:S(2)}, u32[]{:S(2)}) collective-permute-start(bf16[2,4,2,32,256]{4,3,2,1,0:T(8,128)(2,1)S(1)} %slice.229.refs_0_), channel_id=1, source_target_pairs={{0,7},{1,0},{2,1},{3,2},{4,3},{5,4},{6,5},{7,6},{8,15},{9,8},{10,9... | collective-permute-start | bytes 786440 | tf_op jit(solution)/shard_map/inverse_a_z/ppermute | solution.py:38
  41.6 10.8 %collective-permute-done.5.refs_7_ = bf16[2,4,2,32,256]{4,3,2,1,0:T(8,128)(2,1)S(1)} collective-permute-done((bf16[2,4,2,32,256]{4,3,2,1,0:T(8,128)(2,1)S(1)}, bf16[2,4,2,32,256]{4,3,2,1,0:T(8,128)(2,1)S(1)}, u32[]{:S(2)}, u32[]{:S(2)}) %collective-permute-start.5) | collective-permute-done | bytes 262176 | tf_op jit(solution)/shard_map/inverse_a_z/ppermute | solution.py:38
  52.3 2.0 %collective-permute-start.6 = (bf16[2,4,2,32,256]{4,3,2,1,0:T(8,128)(2,1)S(1)}, bf16[2,4,2,32,256]{4,3,2,1,0:T(8,128)(2,1)S(1)}, u32[]{:S(2)}, u32[]{:S(2)}) collective-permute-start(bf16[2,4,2,32,256]{4,3,2,1,0:T(8,128)(2,1)S(1)} %collective-permute-done.4.refs_1_), channel_id=1, source_target_pairs={{0,7},{1,0},{2,1},{3,2},{4,3},{5,4},{6,5},{7,6},{8,15},{9,8},{10,9... | collective-permute-start | bytes 786440 | tf_op jit(solution)/shard_map/inverse_a_z/ppermute | solution.py:38
  54.3 2.6 %collective-permute-start.13 = (bf16[512,1024]{1,0:T(8,128)(2,1)}, bf16[512,1024]{1,0:T(8,128)(2,1)}, u32[]{:S(2)}, u32[]{:S(2)}) collective-permute-start(bf16[512,1024]{1,0:T(8,128)(2,1)} %get-tuple-element.19), channel_id=1, source_target_pairs={{0,64},{64,0},{1,65},{65,1},{2,66},{66,2},{3,67},{67,3},{4,68},{68... | collective-permute-start | bytes 3145736 | tf_op jit(solution)/shard_map/top_row/ppermute | solution.py:38
  57.0 6.0 %collective-permute-done.6.refs_2_ = bf16[2,4,2,32,256]{4,3,2,1,0:T(8,128)(2,1)S(1)} collective-permute-done((bf16[2,4,2,32,256]{4,3,2,1,0:T(8,128)(2,1)S(1)}, bf16[2,4,2,32,256]{4,3,2,1,0:T(8,128)(2,1)S(1)}, u32[]{:S(2)}, u32[]{:S(2)}) %collective-permute-start.6) | collective-permute-done | bytes 262176 | tf_op jit(solution)/shard_map/inverse_a_z/ppermute | solution.py:38
  62.9 1.7 collective-permute-start.15
  65.5 1.6 collective-permute-start.7
  67.1 1.9 %slice.234 = bf16[2,2,256,256]{3,2,1,0:T(8,128)(2,1)} slice(bf16[2,2,256,768]{3,2,1,0:T(8,128)(2,1)} %all-gather.3.cloned.1.call-done), slice={[0:2], [0:2], [0:256], [0:256]} | slice | bytes 1048576 | tf_op jit(solution)/shard_map/slice | solution.py:156
  69.1 2.7 %collective-permute-start.10 = (bf16[2,2,256,256]{3,2,1,0:T(8,128)(2,1)}, bf16[2,2,256,256]{3,2,1,0:T(8,128)(2,1)}, u32[]{:S(2)}, u32[]{:S(2)}) collective-permute-start(bf16[2,2,256,256]{3,2,1,0:T(8,128)(2,1)} %slice.234), channel_id=1, source_target_pairs={{0,48},{16,0},{32,16},{48,32},{1,49},{17,1},{33,17},{49,33},{2,50}... | collective-permute-start | bytes 1572872 | tf_op jit(solution)/shard_map/inverse_b_y/ppermute | solution.py:38
  71.7 3.8 %pad_maximum_fusion.1 = bf16[4,512,1024]{2,1,0:T(8,128)(2,1)} fusion(bf16[1,512,1024]{2,1,0:T(8,128)(2,1)} %bitcast.9, bf16[1,512,1024]{2,1,0:T(8,128)(2,1)} %bitcast.8, bf16[1,512,1024]{2,1,0:T(8,128)(2,1)} %bitcast.7, bf16[1,512,1024]{2,1,0:T(8,128)(2,1)} %bitcast.6), kind=kLoop, calls=%fused_computation.9 | loop fusion | flops 6291456 | bytes 8388608 | tf_op jit(solution)/shard_map/top_row/stack | solution.py:164
  75.5 1.5 collective-permute-start.8
  77.4 1.1 fusion.80
  78.5 1.4 slice.258
  79.9 3.8 %collective-permute-done.11 = bf16[2,2,256,256]{3,2,1,0:T(8,128)(2,1)S(1)} collective-permute-done((bf16[2,2,256,256]{3,2,1,0:T(8,128)(2,1)}, bf16[2,2,256,256]{3,2,1,0:T(8,128)(2,1)S(1)}, u32[]{:S(2)}, u32[]{:S(2)}) %collective-permute-start.11) | collective-permute-done | bytes 524320 | tf_op jit(solution)/shard_map/inverse_b_y/ppermute | solution.py:38
  83.7 2.7 %collective-permute-start.24 = (bf16[2,2,256,512]{3,2,1,0:T(8,128)(2,1)S(1)}, bf16[2,2,256,512]{3,2,1,0:T(8,128)(2,1)S(1)}, u32[]{:S(2)}, u32[]{:S(2)}) collective-permute-start(bf16[2,2,256,512]{3,2,1,0:T(8,128)(2,1)S(1)} %slice.258), channel_id=1, source_target_pairs={{0,48},{16,0},{32,16},{48,32},{1,49},{17,1},{33,17},{49,33},{2,50}... | collective-permute-start | bytes 3145736 | tf_op jit(solution)/shard_map/factor_b_y/ppermute | solution.py:38
  86.6 1.1 fusion.82
  87.7 2.7 %collective-permute-start.17 = (bf16[2,256,256]{2,1,0:T(8,128)(2,1)S(1)}, bf16[2,256,256]{2,1,0:T(8,128)(2,1)S(1)}, u32[]{:S(2)}, u32[]{:S(2)}) collective-permute-start(bf16[2,256,256]{2,1,0:T(8,128)(2,1)S(1)} %get-tuple-element.66), channel_id=1, source_target_pairs={{0,48},{16,0},{32,16},{48,32},{1,49},{17,1},{33,17},{49,33},{2,50}... | collective-permute-start | bytes 786440 | tf_op jit(solution)/shard_map/inverse_b_y/ppermute | solution.py:38
  90.5 1.7 collective-permute-start.12
  94.0 10.8 %collective-permute-done.12.refs_4_ = bf16[2,4,2,32,256]{4,3,2,1,0:T(8,128)(2,1)S(1)} collective-permute-done((bf16[2,4,2,32,256]{4,3,2,1,0:T(8,128)(2,1)S(1)}, bf16[2,4,2,32,256]{4,3,2,1,0:T(8,128)(2,1)S(1)}, u32[]{:S(2)}, u32[]{:S(2)}) %collective-permute-start.12) | collective-permute-done | bytes 262176 | tf_op jit(solution)/shard_map/inverse_a_z/ppermute | solution.py:38
  106.2 1.3 convolution_add_fusion.4
  107.4 1.3 convolution_add_fusion.5
  109.9 1.4 collective-permute-start.19
  111.3 1.9 %collective-permute-done.17 = bf16[2,256,256]{2,1,0:T(8,128)(2,1)S(1)} collective-permute-done((bf16[2,256,256]{2,1,0:T(8,128)(2,1)S(1)}, bf16[2,256,256]{2,1,0:T(8,128)(2,1)S(1)}, u32[]{:S(2)}, u32[]{:S(2)}) %collective-permute-start.17) | collective-permute-done | bytes 262176 | tf_op jit(solution)/shard_map/inverse_b_y/ppermute | solution.py:38
  113.2 2.2 %collective-permute-start.18 = (bf16[256,1024]{1,0:T(8,128)(2,1)}, bf16[256,1024]{1,0:T(8,128)(2,1)}, u32[]{:S(2)}, u32[]{:S(2)}) collective-permute-start(bf16[256,1024]{1,0:T(8,128)(2,1)} %get-tuple-element.61), channel_id=1, source_target_pairs={{0,64},{64,0},{1,65},{65,1},{2,66},{66,2},{3,67},{67,3},{4,68},{68... | collective-permute-start | bytes 1572872 | tf_op jit(solution)/shard_map/solved_a_row/ppermute | solution.py:38
  116.8 1.3 bitcast_select_fusion.2
  120.5 12.7 %collective-permute-start.22 = (bf16[256,1024]{1,0:T(8,128)(2,1)S(1)}, bf16[256,1024]{1,0:T(8,128)(2,1)S(1)}, u32[]{:S(2)}, u32[]{:S(2)}) collective-permute-start(bf16[256,1024]{1,0:T(8,128)(2,1)S(1)} %get-tuple-element.59), channel_id=1, source_target_pairs={{0,128},{128,0},{1,129},{129,1},{2,130},{130,2},{3,131},{131,3},{4... | collective-permute-start | bytes 1572872 | tf_op jit(solution)/shard_map/solved_b_row/ppermute | solution.py:38
  133.3 2.9 %collective-permute-start.20 = (bf16[256,1024]{1,0:T(8,128)(2,1)}, bf16[256,1024]{1,0:T(8,128)(2,1)S(1)}, u32[]{:S(2)}, u32[]{:S(2)}) collective-permute-start(bf16[256,1024]{1,0:T(8,128)(2,1)} %collective-permute-done.19), channel_id=1, source_target_pairs={{0,64},{64,0},{1,65},{65,1},{2,66},{66,2},{3,67},{67,3},{4,68},{68... | collective-permute-start | bytes 1572872 | tf_op jit(solution)/shard_map/solved_a_row/ppermute | solution.py:38
  136.2 1.5 pad_maximum_fusion.4
  140.4 2.2 %collective-permute-done.22 = bf16[256,1024]{1,0:T(8,128)(2,1)S(1)} collective-permute-done((bf16[256,1024]{1,0:T(8,128)(2,1)S(1)}, bf16[256,1024]{1,0:T(8,128)(2,1)S(1)}, u32[]{:S(2)}, u32[]{:S(2)}) %collective-permute-start.22) | collective-permute-done | bytes 524320 | tf_op jit(solution)/shard_map/solved_b_row/ppermute | solution.py:38
  142.6 5.7 %collective-permute-start.27 = (bf16[2,256,512]{2,1,0:T(8,128)(2,1)}, bf16[2,256,512]{2,1,0:T(8,128)(2,1)}, u32[]{:S(2)}, u32[]{:S(2)}) collective-permute-start(bf16[2,256,512]{2,1,0:T(8,128)(2,1)} %slice_bitcast_fusion.4), channel_id=1, source_target_pairs={{0,48},{16,0},{32,16},{48,32},{1,49},{17,1},{33,17},{49,33},{2,50}... | collective-permute-start | bytes 1572872 | tf_op jit(solution)/shard_map/factor_b_y/ppermute | solution.py:38
  148.3 1.0 collective-permute-start.23
  149.3 1.6 maximum_bitcast_fusion
  161.1 2.3 %fusion.87 = f32[512,1024]{1,0:T(8,128)S(1)} fusion(bf16[2048,512]{1,0:T(8,128)(2,1)S(1)} %bitcast.186, bf16[2048,1024]{1,0:T(8,128)(2,1)S(1)} %bitcast.183), kind=kOutput, calls=%fused_computation.144 | convolution fusion | flops 2147483648 | bytes 8388608 | tf_op jit(solution)/shard_map/update_a/dot_general | solution.py:106
  164.1 2.3 %fusion.88 = f32[512,1024]{1,0:T(8,128)S(1)} fusion(bf16[2048,512]{1,0:T(8,128)(2,1)S(1)} %bitcast.185, bf16[2048,1024]{1,0:T(8,128)(2,1)S(1)} %bitcast.184), kind=kOutput, calls=%fused_computation.145 | convolution fusion | flops 2147483648 | bytes 8388608 | tf_op jit(solution)/shard_map/update_a/dot_general | solution.py:106
  167.8 2.6 %convolution_add_fusion = f32[512,1024]{1,0:T(8,128)S(1)} fusion(f32[512,1024]{1,0:T(8,128)} %copy-done.1, bf16[512,512]{1,0:T(8,128)(2,1)} %bitcast.67, bf16[512,1024]{1,0:T(8,128)(2,1)S(1)} %bitcast.181), kind=kOutput, calls=%fused_computation.24 | convolution fusion | flops 537395200 | bytes 5767168 | tf_op jit(solution)/shard_map/update_b/dot_general | solution.py:106
  170.5 1.9 %convolution_add_fusion.1 = f32[512,1024]{1,0:T(8,128)S(1)} fusion(f32[512,1024]{1,0:T(8,128)S(1)} %bitcast_add_fusion.2, bf16[512,512]{1,0:T(8,128)(2,1)} %bitcast.65, bf16[512,1024]{1,0:T(8,128)(2,1)S(1)} %bitcast.182), kind=kOutput, calls=%fused_computation.25 | convolution fusion | flops 537395200 | bytes 5767168 | tf_op jit(solution)/shard_map/update_b/dot_general | solution.py:106
  172.9 1.6 fusion.15
  174.9 2.5 %pad_maximum_fusion.2 = f32[2,1024,512]{2,1,0:T(8,128)} fusion(f32[1,1024,512]{2,1,0:T(8,128)S(1)} %get-tuple-element.77, f32[1,1024,512]{2,1,0:T(8,128)S(1)} %get-tuple-element.76), kind=kLoop, calls=%fused_computation.10 | loop fusion | flops 1048576 | bytes 8388608 | tf_op jit(solution)/shard_map/stack | solution.py:218
  (112 shorter events, 28.5 us)
Async XLA Ops:
  7.2 10.0 %copy-start.14 = (f32[2,512,512]{2,1,0:T(8,128)S(1)}, f32[2,512,512]{2,1,0:T(8,128)}, u32[]{:S(2)}) copy-start(f32[2,512,512]{2,1,0:T(8,128)} %param.5) | copy-start | bytes 6291460
  7.2 60.0 %all-gather.3.cloned.1.call-start = ((), (), s32[]{:S(2)}) async-start(), calls=%async_computation | async-start | bytes 1769472 | tf_op jit(solution)/shard_map/b_z/all_gather | solution.py:153
  9.1 7.2 %collective-permute-start = (bf16[2,32,1536]{2,1,0:T(8,128)(2,1)S(1)}, bf16[2,32,1536]{2,1,0:T(8,128)(2,1)S(1)}, u32[]{:S(2)}, u32[]{:S(2)}) collective-permute-start(bf16[2,32,1536]{2,1,0:T(8,128)(2,1)S(1)} %constant_dynamic-update-slice_fusion), channel_id=1, source_target_pairs={{0,8},{8,0},{1,9},{9,1},{2,10},{10,2},{3,11},{11,3},{4,12},{12,4},... | collective-permute-start | bytes 589832 | tf_op jit(solution)/shard_map/panel_x/ppermute | solution.py:38
  17.2 131.2 %all-gather.5.cloned.1.call-start = ((), (), s32[]{:S(2)}) async-start(), calls=%async_computation.1 | async-start | bytes 4718592 | tf_op jit(solution)/shard_map/factor_a_z/all_gather | solution.py:168
  18.8 44.1 %collective-permute-start.14 = (bf16[512,1024]{1,0:T(8,128)(2,1)}, bf16[512,1024]{1,0:T(8,128)(2,1)}, u32[]{:S(2)}, u32[]{:S(2)}) collective-permute-start(bf16[512,1024]{1,0:T(8,128)(2,1)} %get-tuple-element.19), channel_id=1, source_target_pairs={{0,128},{128,0},{1,129},{129,1},{2,130},{130,2},{3,131},{131,3},{4... | collective-permute-start | bytes 3145736 | tf_op jit(solution)/shard_map/top_row/ppermute | solution.py:38
  21.0 7.3 %collective-permute-start.1 = (bf16[2,2,32,768]{3,2,1,0:T(8,128)(2,1)S(1)}, bf16[2,2,32,768]{3,2,1,0:T(8,128)(2,1)S(1)}, u32[]{:S(2)}, u32[]{:S(2)}) collective-permute-start(bf16[2,2,32,768]{3,2,1,0:T(8,128)(2,1)S(1)} %pad_maximum_fusion.8.refs_0_), channel_id=1, source_target_pairs={{0,48},{16,0},{32,16},{48,32},{1,49},{17,1},{33,17},{49,33},{2,50}... | collective-permute-start | bytes 589832 | tf_op jit(solution)/shard_map/a_y/ppermute | solution.py:38
  23.8 6.1 %collective-permute-start.2 = (bf16[2,2,32,768]{3,2,1,0:T(8,128)(2,1)S(1)}, bf16[2,2,32,768]{3,2,1,0:T(8,128)(2,1)S(1)}, u32[]{:S(2)}, u32[]{:S(2)}) collective-permute-start(bf16[2,2,32,768]{3,2,1,0:T(8,128)(2,1)S(1)} %pad_maximum_fusion.8.refs_0_), channel_id=1, source_target_pairs={{0,32},{16,48},{32,0},{48,16},{1,33},{17,49},{33,1},{49,17},{2,34}... | collective-permute-start | bytes 589832 | tf_op jit(solution)/shard_map/a_y/ppermute | solution.py:38
  24.1 11.6 %collective-permute-start.3 = (bf16[2,2,32,768]{3,2,1,0:T(8,128)(2,1)S(1)}, bf16[2,2,32,768]{3,2,1,0:T(8,128)(2,1)S(1)}, u32[]{:S(2)}, u32[]{:S(2)}) collective-permute-start(bf16[2,2,32,768]{3,2,1,0:T(8,128)(2,1)S(1)} %pad_maximum_fusion.8.refs_0_), channel_id=1, source_target_pairs={{0,16},{16,32},{32,48},{48,0},{1,17},{17,33},{33,49},{49,1},{2,18}... | collective-permute-start | bytes 589832 | tf_op jit(solution)/shard_map/a_y/ppermute | solution.py:38
  35.8 16.5 %collective-permute-start.5 = (bf16[2,4,2,32,256]{4,3,2,1,0:T(8,128)(2,1)S(1)}, bf16[2,4,2,32,256]{4,3,2,1,0:T(8,128)(2,1)S(1)}, u32[]{:S(2)}, u32[]{:S(2)}) collective-permute-start(bf16[2,4,2,32,256]{4,3,2,1,0:T(8,128)(2,1)S(1)} %slice.229.refs_0_), channel_id=1, source_target_pairs={{0,1},{1,2},{2,3},{3,4},{4,5},{5,6},{6,7},{7,0},{8,9},{9,10},{10,1... | collective-permute-start | bytes 786440 | tf_op jit(solution)/shard_map/inverse_a_z/ppermute | solution.py:38
  37.5 14.8 %collective-permute-start.4 = (bf16[2,4,2,32,256]{4,3,2,1,0:T(8,128)(2,1)S(1)}, bf16[2,4,2,32,256]{4,3,2,1,0:T(8,128)(2,1)S(1)}, u32[]{:S(2)}, u32[]{:S(2)}) collective-permute-start(bf16[2,4,2,32,256]{4,3,2,1,0:T(8,128)(2,1)S(1)} %slice.229.refs_0_), channel_id=1, source_target_pairs={{0,7},{1,0},{2,1},{3,2},{4,3},{5,4},{6,5},{7,6},{8,15},{9,8},{10,9... | collective-permute-start | bytes 786440 | tf_op jit(solution)/shard_map/inverse_a_z/ppermute | solution.py:38
  52.3 10.6 %collective-permute-start.6 = (bf16[2,4,2,32,256]{4,3,2,1,0:T(8,128)(2,1)S(1)}, bf16[2,4,2,32,256]{4,3,2,1,0:T(8,128)(2,1)S(1)}, u32[]{:S(2)}, u32[]{:S(2)}) collective-permute-start(bf16[2,4,2,32,256]{4,3,2,1,0:T(8,128)(2,1)S(1)} %collective-permute-done.4.refs_1_), channel_id=1, source_target_pairs={{0,7},{1,0},{2,1},{3,2},{4,3},{5,4},{6,5},{7,6},{8,15},{9,8},{10,9... | collective-permute-start | bytes 786440 | tf_op jit(solution)/shard_map/inverse_a_z/ppermute | solution.py:38
  54.3 17.4 %collective-permute-start.13 = (bf16[512,1024]{1,0:T(8,128)(2,1)}, bf16[512,1024]{1,0:T(8,128)(2,1)}, u32[]{:S(2)}, u32[]{:S(2)}) collective-permute-start(bf16[512,1024]{1,0:T(8,128)(2,1)} %get-tuple-element.19), channel_id=1, source_target_pairs={{0,64},{64,0},{1,65},{65,1},{2,66},{66,2},{3,67},{67,3},{4,68},{68... | collective-permute-start | bytes 3145736 | tf_op jit(solution)/shard_map/top_row/ppermute | solution.py:38
  62.9 8.8 %collective-permute-start.15 = (bf16[512,1024]{1,0:T(8,128)(2,1)}, bf16[512,1024]{1,0:T(8,128)(2,1)}, u32[]{:S(2)}, u32[]{:S(2)}) collective-permute-start(bf16[512,1024]{1,0:T(8,128)(2,1)} %collective-permute-done.14), channel_id=1, source_target_pairs={{0,64},{64,0},{1,65},{65,1},{2,66},{66,2},{3,67},{67,3},{4,68},{68... | collective-permute-start | bytes 3145736 | tf_op jit(solution)/shard_map/top_row/ppermute | solution.py:38
  65.5 10.0 %collective-permute-start.7 = (bf16[2,4,2,32,256]{4,3,2,1,0:T(8,128)(2,1)S(1)}, bf16[2,4,2,32,256]{4,3,2,1,0:T(8,128)(2,1)S(1)}, u32[]{:S(2)}, u32[]{:S(2)}) collective-permute-start(bf16[2,4,2,32,256]{4,3,2,1,0:T(8,128)(2,1)S(1)} %collective-permute-done.5.refs_7_), channel_id=1, source_target_pairs={{0,1},{1,2},{2,3},{3,4},{4,5},{5,6},{6,7},{7,0},{8,9},{9,10},{10,1... | collective-permute-start | bytes 786440 | tf_op jit(solution)/shard_map/inverse_a_z/ppermute | solution.py:38
  69.1 14.7 %collective-permute-start.11 = (bf16[2,2,256,256]{3,2,1,0:T(8,128)(2,1)}, bf16[2,2,256,256]{3,2,1,0:T(8,128)(2,1)S(1)}, u32[]{:S(2)}, u32[]{:S(2)}) collective-permute-start(bf16[2,2,256,256]{3,2,1,0:T(8,128)(2,1)} %slice.234), channel_id=1, source_target_pairs={{0,16},{16,32},{32,48},{48,0},{1,17},{17,33},{33,49},{49,1},{2,18}... | collective-permute-start | bytes 1572872 | tf_op jit(solution)/shard_map/inverse_b_y/ppermute | solution.py:38
  69.1 14.7 %collective-permute-start.10 = (bf16[2,2,256,256]{3,2,1,0:T(8,128)(2,1)}, bf16[2,2,256,256]{3,2,1,0:T(8,128)(2,1)}, u32[]{:S(2)}, u32[]{:S(2)}) collective-permute-start(bf16[2,2,256,256]{3,2,1,0:T(8,128)(2,1)} %slice.234), channel_id=1, source_target_pairs={{0,48},{16,0},{32,16},{48,32},{1,49},{17,1},{33,17},{49,33},{2,50}... | collective-permute-start | bytes 1572872 | tf_op jit(solution)/shard_map/inverse_b_y/ppermute | solution.py:38
  75.5 12.2 %collective-permute-start.8 = (bf16[2,4,2,32,256]{4,3,2,1,0:T(8,128)(2,1)S(1)}, bf16[2,4,2,32,256]{4,3,2,1,0:T(8,128)(2,1)S(1)}, u32[]{:S(2)}, u32[]{:S(2)}) collective-permute-start(bf16[2,4,2,32,256]{4,3,2,1,0:T(8,128)(2,1)S(1)} %collective-permute-done.6.refs_2_), channel_id=1, source_target_pairs={{0,7},{1,0},{2,1},{3,2},{4,3},{5,4},{6,5},{7,6},{8,15},{9,8},{10,9... | collective-permute-start | bytes 786440 | tf_op jit(solution)/shard_map/inverse_a_z/ppermute | solution.py:38
  77.0 13.4 %collective-permute-start.9 = (bf16[2,4,2,32,256]{4,3,2,1,0:T(8,128)(2,1)S(1)}, bf16[2,4,2,32,256]{4,3,2,1,0:T(8,128)(2,1)S(1)}, u32[]{:S(2)}, u32[]{:S(2)}) collective-permute-start(bf16[2,4,2,32,256]{4,3,2,1,0:T(8,128)(2,1)S(1)} %collective-permute-done.7.refs_6_), channel_id=1, source_target_pairs={{0,1},{1,2},{2,3},{3,4},{4,5},{5,6},{6,7},{7,0},{8,9},{9,10},{10,1... | collective-permute-start | bytes 786440 | tf_op jit(solution)/shard_map/inverse_a_z/ppermute | solution.py:38
  78.5 13.7 %copy-start = (bf16[4,512,1024]{2,1,0:T(8,128)(2,1)S(1)}, bf16[4,512,1024]{2,1,0:T(8,128)(2,1)}, u32[]{:S(2)}) copy-start(bf16[4,512,1024]{2,1,0:T(8,128)(2,1)} %pad_maximum_fusion.1) | copy-start | bytes 12582916
  79.9 12.7 %copy-start.2 = (bf16[2,2,256,512]{3,2,1,0:T(8,128)(2,1)}, bf16[2,2,256,512]{3,2,1,0:T(8,128)(2,1)S(1)}, u32[]{:S(2)}) copy-start(bf16[2,2,256,512]{3,2,1,0:T(8,128)(2,1)S(1)} %slice.258) | copy-start | bytes 3145732
  83.7 54.9 %collective-permute-start.24 = (bf16[2,2,256,512]{3,2,1,0:T(8,128)(2,1)S(1)}, bf16[2,2,256,512]{3,2,1,0:T(8,128)(2,1)S(1)}, u32[]{:S(2)}, u32[]{:S(2)}) collective-permute-start(bf16[2,2,256,512]{3,2,1,0:T(8,128)(2,1)S(1)} %slice.258), channel_id=1, source_target_pairs={{0,48},{16,0},{32,16},{48,32},{1,49},{17,1},{33,17},{49,33},{2,50}... | collective-permute-start | bytes 3145736 | tf_op jit(solution)/shard_map/factor_b_y/ppermute | solution.py:38
  86.4 51.3 %collective-permute-start.25 = (bf16[2,2,256,512]{3,2,1,0:T(8,128)(2,1)S(1)}, bf16[2,2,256,512]{3,2,1,0:T(8,128)(2,1)S(1)}, u32[]{:S(2)}, u32[]{:S(2)}) collective-permute-start(bf16[2,2,256,512]{3,2,1,0:T(8,128)(2,1)S(1)} %slice.258), channel_id=1, source_target_pairs={{0,16},{16,32},{32,48},{48,0},{1,17},{17,33},{33,49},{49,1},{2,18}... | collective-permute-start | bytes 3145736 | tf_op jit(solution)/shard_map/factor_b_y/ppermute | solution.py:38
  86.5 29.8 %collective-permute-start.16 = (bf16[2,256,256]{2,1,0:T(8,128)(2,1)S(1)}, bf16[2,256,256]{2,1,0:T(8,128)(2,1)S(1)}, u32[]{:S(2)}, u32[]{:S(2)}) collective-permute-start(bf16[2,256,256]{2,1,0:T(8,128)(2,1)S(1)} %get-tuple-element.63), channel_id=1, source_target_pairs={{0,16},{16,32},{32,48},{48,0},{1,17},{17,33},{33,49},{49,1},{2,18}... | collective-permute-start | bytes 786440 | tf_op jit(solution)/shard_map/inverse_b_y/ppermute | solution.py:38
  87.7 25.5 %collective-permute-start.17 = (bf16[2,256,256]{2,1,0:T(8,128)(2,1)S(1)}, bf16[2,256,256]{2,1,0:T(8,128)(2,1)S(1)}, u32[]{:S(2)}, u32[]{:S(2)}) collective-permute-start(bf16[2,256,256]{2,1,0:T(8,128)(2,1)S(1)} %get-tuple-element.66), channel_id=1, source_target_pairs={{0,48},{16,0},{32,16},{48,32},{1,49},{17,1},{33,17},{49,33},{2,50}... | collective-permute-start | bytes 786440 | tf_op jit(solution)/shard_map/inverse_b_y/ppermute | solution.py:38
  90.5 14.3 %collective-permute-start.12 = (bf16[2,4,2,32,256]{4,3,2,1,0:T(8,128)(2,1)S(1)}, bf16[2,4,2,32,256]{4,3,2,1,0:T(8,128)(2,1)S(1)}, u32[]{:S(2)}, u32[]{:S(2)}) collective-permute-start(bf16[2,4,2,32,256]{4,3,2,1,0:T(8,128)(2,1)S(1)} %collective-permute-done.9.refs_5_), channel_id=1, source_target_pairs={{0,1},{1,2},{2,3},{3,4},{4,5},{5,6},{6,7},{7,0},{8,9},{9,10},{10,1... | collective-permute-start | bytes 786440 | tf_op jit(solution)/shard_map/inverse_a_z/ppermute | solution.py:38
  109.9 23.4 %collective-permute-start.19 = (bf16[256,1024]{1,0:T(8,128)(2,1)}, bf16[256,1024]{1,0:T(8,128)(2,1)}, u32[]{:S(2)}, u32[]{:S(2)}) collective-permute-start(bf16[256,1024]{1,0:T(8,128)(2,1)} %get-tuple-element.61), channel_id=1, source_target_pairs={{0,128},{128,0},{1,129},{129,1},{2,130},{130,2},{3,131},{131,3},{4... | collective-permute-start | bytes 1572872 | tf_op jit(solution)/shard_map/solved_a_row/ppermute | solution.py:38
  113.2 35.1 %collective-permute-start.18 = (bf16[256,1024]{1,0:T(8,128)(2,1)}, bf16[256,1024]{1,0:T(8,128)(2,1)}, u32[]{:S(2)}, u32[]{:S(2)}) collective-permute-start(bf16[256,1024]{1,0:T(8,128)(2,1)} %get-tuple-element.61), channel_id=1, source_target_pairs={{0,64},{64,0},{1,65},{65,1},{2,66},{66,2},{3,67},{67,3},{4,68},{68... | collective-permute-start | bytes 1572872 | tf_op jit(solution)/shard_map/solved_a_row/ppermute | solution.py:38
  120.5 22.1 %collective-permute-start.22 = (bf16[256,1024]{1,0:T(8,128)(2,1)S(1)}, bf16[256,1024]{1,0:T(8,128)(2,1)S(1)}, u32[]{:S(2)}, u32[]{:S(2)}) collective-permute-start(bf16[256,1024]{1,0:T(8,128)(2,1)S(1)} %get-tuple-element.59), channel_id=1, source_target_pairs={{0,128},{128,0},{1,129},{129,1},{2,130},{130,2},{3,131},{131,3},{4... | collective-permute-start | bytes 1572872 | tf_op jit(solution)/shard_map/solved_b_row/ppermute | solution.py:38
  133.3 16.0 %collective-permute-start.20 = (bf16[256,1024]{1,0:T(8,128)(2,1)}, bf16[256,1024]{1,0:T(8,128)(2,1)S(1)}, u32[]{:S(2)}, u32[]{:S(2)}) collective-permute-start(bf16[256,1024]{1,0:T(8,128)(2,1)} %collective-permute-done.19), channel_id=1, source_target_pairs={{0,64},{64,0},{1,65},{65,1},{2,66},{66,2},{3,67},{67,3},{4,68},{68... | collective-permute-start | bytes 1572872 | tf_op jit(solution)/shard_map/solved_a_row/ppermute | solution.py:38
  137.7 2.7 %copy-start.8 = (bf16[2,2,256,512]{3,2,1,0:T(8,128)(2,1)}, bf16[2,2,256,512]{3,2,1,0:T(8,128)(2,1)S(1)}, u32[]{:S(2)}) copy-start(bf16[2,2,256,512]{3,2,1,0:T(8,128)(2,1)S(1)} %collective-permute-done.25) | copy-start | bytes 3145732
  137.7 14.5 %collective-permute-start.21 = (bf16[256,1024]{1,0:T(8,128)(2,1)S(1)}, bf16[256,1024]{1,0:T(8,128)(2,1)S(1)}, u32[]{:S(2)}, u32[]{:S(2)}) collective-permute-start(bf16[256,1024]{1,0:T(8,128)(2,1)S(1)} %get-tuple-element.59), channel_id=1, source_target_pairs={{0,64},{64,0},{1,65},{65,1},{2,66},{66,2},{3,67},{67,3},{4,68},{68... | collective-permute-start | bytes 1572872 | tf_op jit(solution)/shard_map/solved_b_row/ppermute | solution.py:38
  138.6 1.0 copy-start.4
  138.6 29.1 %collective-permute-start.26 = (bf16[2,256,512]{2,1,0:T(8,128)(2,1)}, bf16[2,256,512]{2,1,0:T(8,128)(2,1)}, u32[]{:S(2)}, u32[]{:S(2)}) collective-permute-start(bf16[2,256,512]{2,1,0:T(8,128)(2,1)} %slice_bitcast_fusion.5), channel_id=1, source_target_pairs={{0,16},{16,32},{32,48},{48,0},{1,17},{17,33},{33,49},{49,1},{2,18}... | collective-permute-start | bytes 1572872 | tf_op jit(solution)/shard_map/factor_b_y/ppermute | solution.py:38
  142.6 25.2 %collective-permute-start.27 = (bf16[2,256,512]{2,1,0:T(8,128)(2,1)}, bf16[2,256,512]{2,1,0:T(8,128)(2,1)}, u32[]{:S(2)}, u32[]{:S(2)}) collective-permute-start(bf16[2,256,512]{2,1,0:T(8,128)(2,1)} %slice_bitcast_fusion.4), channel_id=1, source_target_pairs={{0,48},{16,0},{32,16},{48,32},{1,49},{17,1},{33,17},{49,33},{2,50}... | collective-permute-start | bytes 1572872 | tf_op jit(solution)/shard_map/factor_b_y/ppermute | solution.py:38
  148.3 3.9 %collective-permute-start.23 = (bf16[256,1024]{1,0:T(8,128)(2,1)S(1)}, bf16[256,1024]{1,0:T(8,128)(2,1)S(1)}, u32[]{:S(2)}, u32[]{:S(2)}) collective-permute-start(bf16[256,1024]{1,0:T(8,128)(2,1)S(1)} %collective-permute-done.22), channel_id=1, source_target_pairs={{0,64},{64,0},{1,65},{65,1},{2,66},{66,2},{3,67},{67,3},{4,68},{68... | collective-permute-start | bytes 1572872 | tf_op jit(solution)/shard_map/solved_b_row/ppermute | solution.py:38
  149.3 2.5 %copy-start.6 = (bf16[2,4,2,256,512]{4,3,2,1,0:T(8,128)(2,1)S(1)}, bf16[2,4,2,256,512]{4,3,2,1,0:T(8,128)(2,1)}, u32[]{:S(2)}) copy-start(bf16[2,4,2,256,512]{4,3,2,1,0:T(8,128)(2,1)} %all-gather.5.cloned.1.call-done) | copy-start | bytes 12582916
  152.5 1.2 copy-start.3
  155.2 1.2 copy-start.5
  156.4 1.2 copy-start.9
  160.4 3.0 %copy-start.1 = (f32[512,1024]{1,0:T(8,128)}, f32[512,1024]{1,0:T(8,128)S(1)}, u32[]{:S(2)}) copy-start(f32[512,1024]{1,0:T(8,128)S(1)} %bitcast_add_fusion) | copy-start | bytes 6291460
  163.5 3.0 %copy-start.10 = (f32[512,1024]{1,0:T(8,128)}, f32[512,1024]{1,0:T(8,128)S(1)}, u32[]{:S(2)}) copy-start(f32[512,1024]{1,0:T(8,128)S(1)} %fusion.87) | copy-start | bytes 6291460
  166.5 1.3 copy-start.12
  167.8 4.6 %copy-start.11 = (f32[512,1024]{1,0:T(8,128)S(1)}, f32[512,1024]{1,0:T(8,128)}, u32[]{:S(2)}) copy-start(f32[512,1024]{1,0:T(8,128)} %copy-done.10) | copy-start | bytes 6291460
  167.8 4.6 %copy-start.13 = (f32[512,1024]{1,0:T(8,128)S(1)}, f32[512,1024]{1,0:T(8,128)}, u32[]{:S(2)}) copy-start(f32[512,1024]{1,0:T(8,128)} %copy-done.12) | copy-start | bytes 6291460
  170.4 2.4 %copy-start.7 = (f32[2,1024,512]{2,1,0:T(8,128)S(1)}, f32[2,1024,512]{2,1,0:T(8,128)}, u32[]{:S(2)}) copy-start(f32[2,1024,512]{2,1,0:T(8,128)} %param.7) | copy-start | bytes 12582916
Sparse Core Ops, SparseCore 0:
  17.3 44.0 all-gather.2
  77.5 58.3 all-gather.4
